TPU v7x, 32 devices: a whole 2x2x4 slice. The times are simulated.
32 devices in a mesh: dp: 8 (over z, x), seq: 4 (over y, core).
Axes of the slice: x: 2, y: 2, z: 4, core: 2. Of those that a mesh axis runs over, the one named last changes fastest.
Arguments:
- layer_input: bfloat16 [16, 2048, 768], P('dp', 'seq'), may hold values from -6 to 6
- cotangent: bfloat16 [16, 2048, 768], P('dp', 'seq'), may hold values from -6 to 6
- norm_gain1: bfloat16 [768], P('dp'), may hold values from 0.099609375 to 1.8984375
- w_qkv: bfloat16 [768, 2304], P('dp'), may hold values from -0.21875 to 0.21875
- w_out: bfloat16 [768, 768], P('dp'), may hold values from -6 to 6
- norm_gain2: bfloat16 [768], P('dp'), may hold values from 0.099609375 to 1.8984375
- w_in: bfloat16 [768, 2304], P('dp'), may hold values from -0.21875 to 0.21875
- w_down: bfloat16 [1152, 768], P(None, 'dp'), may hold values from -0.1875 to 0.1875
Outputs:
- output: bfloat16 [16, 2048, 768], P('dp', 'seq')
- grad_input: float32 [16, 2048, 768], P('dp', 'seq')
- grad_gain1: float32 [768], P('dp')
- grad_qkv: float32 [768, 2304], P('dp')
- grad_out: float32 [768, 768], P('dp')
- grad_gain2: float32 [768], P('dp')
- grad_in: float32 [768, 2304], P('dp')
- grad_down: float32 [1152, 768], P(None, 'dp')
All inputs are finite; a program needn't handle non-finite values.
Results may differ from a plain program's by a relative error of at most 0.017.
Values may be sent and summed in bfloat16 or wider, within the bound.
A program may use at most 128 MiB of HBM per device.

v0:
```python
import jax
import jax.numpy as jnp
from jax import lax
from jax.sharding import PartitionSpec as P

H = 12
HD = 64
FF = 1152


rope_base = 160000.0
norm_eps = 1e-05


def normalize(values):
    centre = values - jnp.mean(values, axis=-1, keepdims=True)
    inverse = lax.rsqrt(jnp.mean(centre * centre, axis=-1, keepdims=True) + norm_eps)
    return (centre * inverse, inverse)


def norm_back(grad_normed, normed, inverse, gain):
    scaled = grad_normed * gain
    first = jnp.mean(scaled, axis=-1, keepdims=True)
    second = jnp.mean(scaled * normed, axis=-1, keepdims=True)
    return inverse * (scaled - first - normed * second)


def rope_tables(positions):
    half = HD // 2
    freqs = rope_base ** (-(jnp.arange(half, dtype=jnp.float32) * 2.0) / HD)
    angles = positions.astype(jnp.float32)[:, None] * freqs[None, :]
    angles = jnp.concatenate([angles, angles], axis=-1)
    return (jnp.cos(angles), jnp.sin(angles))


def rotate(values, cosine, sine):
    half = values.shape[-1] // 2
    turned = jnp.concatenate([-values[..., half:], values[..., :half]], axis=-1)
    return values * cosine[:, None, :] + turned * sine[:, None, :]


def rotate_back(grads, cosine, sine):
    half = grads.shape[-1] // 2
    moved = grads * sine[:, None, :]
    turned = jnp.concatenate([moved[..., half:], -moved[..., :half]], axis=-1)
    return grads * cosine[:, None, :] + turned


def exact_gelu(values):
    return jax.nn.gelu(values, approximate=False)


def contract_rows(left, right):
    return lax.dot_general(
        left, right, (((0,), (0,)), ((), ())), preferred_element_type=jnp.float32
    )


def times_transpose(left, right):
    return lax.dot_general(
        left, right, (((1,), (1,)), ((), ())), preferred_element_type=jnp.float32
    )


def attend_one(query, keys, values, block, scale):
    length, local, size = query.shape
    count = length // block

    def one_block(rows):
        scores = jnp.einsum("qhd,khd->hqk", rows, keys, preferred_element_type=jnp.float32) * scale
        top = jnp.max(scores, axis=-1, keepdims=True)
        weights = jnp.exp(scores - top)
        total = jnp.sum(weights, axis=-1, keepdims=True)
        probs = (weights / total).astype(jnp.bfloat16)
        result = jnp.einsum("hqk,khd->qhd", probs, values, preferred_element_type=jnp.float32)
        return (result.astype(jnp.bfloat16), (top + jnp.log(total))[..., 0])

    outs, logsum = lax.map(one_block, query.reshape(count, block, local, size))
    return (outs.reshape(length, local, size), logsum)


def attend_back(query, keys, values, grad_rows_all, logsum, block, scale):
    length, local, size = query.shape
    count = length // block

    def one_block(carry, pieces):
        rows, grad_rows, log_total = pieces
        grad_keys, grad_values = carry
        scores = jnp.einsum("qhd,khd->hqk", rows, keys, preferred_element_type=jnp.float32) * scale
        probs = jnp.exp(scores - log_total[..., None])
        grad_probs = jnp.einsum(
            "qhd,khd->hqk", grad_rows, values, preferred_element_type=jnp.float32
        )
        inner = jnp.sum(probs * grad_probs, axis=-1, keepdims=True)
        grad_scores = (probs * (grad_probs - inner)).astype(jnp.bfloat16)
        grad_query = (
            jnp.einsum("hqk,khd->qhd", grad_scores, keys, preferred_element_type=jnp.float32)
            * scale
        )
        grad_keys = (
            grad_keys
            + jnp.einsum("hqk,qhd->khd", grad_scores, rows, preferred_element_type=jnp.float32)
            * scale
        )
        grad_values = grad_values + jnp.einsum(
            "hqk,qhd->khd",
            probs.astype(jnp.bfloat16),
            grad_rows,
            preferred_element_type=jnp.float32,
        )
        return ((grad_keys, grad_values), grad_query)

    pieces = (
        query.reshape(count, block, local, size),
        grad_rows_all.reshape(count, block, local, size),
        logsum,
    )
    start = (jnp.zeros(keys.shape, jnp.float32), jnp.zeros(keys.shape, jnp.float32))
    (grad_keys, grad_values), grad_query = lax.scan(one_block, start, pieces)
    return (
        grad_query.reshape(length, local, size).astype(jnp.bfloat16),
        grad_keys.astype(jnp.bfloat16),
        grad_values.astype(jnp.bfloat16),
    )


def shards(layer_input, cotangent, norm_gain1, w_qkv, w_out, norm_gain2, w_in, w_down):
    seq_count, tokens_dev, width = layer_input.shape
    parts = lax.axis_size("seq")
    local_heads = H // parts
    rows = seq_count * tokens_dev
    length = tokens_dev * parts
    block = min(512, length)
    scale = HD ** (-0.5)
    gathered = (
        lax.all_gather(norm_gain1, "dp", axis=0, tiled=True),
        lax.all_gather(w_qkv, "dp", axis=0, tiled=True),
        lax.all_gather(w_out, "dp", axis=0, tiled=True),
        lax.all_gather(norm_gain2, "dp", axis=0, tiled=True),
        lax.all_gather(w_in, "dp", axis=0, tiled=True),
        lax.all_gather(w_down, "dp", axis=1, tiled=True),
    )
    gain_one, proj_qkv, proj_out, gain_two, proj_in, proj_down = gathered
    inputs = layer_input.reshape(rows, width).astype(jnp.float32)
    normed_one, inverse_one = normalize(inputs)
    attn_in = (normed_one * gain_one.astype(jnp.float32)).astype(jnp.bfloat16)
    mixed = jnp.dot(attn_in, proj_qkv, preferred_element_type=jnp.float32).reshape(
        seq_count, tokens_dev, 3, H, HD
    )
    positions = lax.axis_index("seq") * tokens_dev + jnp.arange(tokens_dev, dtype=jnp.int32)
    cosine, sine = rope_tables(positions)
    turned = jnp.stack(
        [
            rotate(mixed[:, :, 0], cosine, sine),
            rotate(mixed[:, :, 1], cosine, sine),
            mixed[:, :, 2],
        ],
        axis=2,
    )
    sending = turned.astype(jnp.bfloat16).reshape(seq_count, tokens_dev, 3, parts, local_heads * HD)
    received = lax.all_to_all(sending, "seq", split_axis=3, concat_axis=1, tiled=True)
    by_head = received.reshape(seq_count, length, 3, local_heads, HD)
    query, keys, values = (by_head[:, :, 0], by_head[:, :, 1], by_head[:, :, 2])
    attended, logsum = lax.map(
        lambda item: attend_one(item[0], item[1], item[2], block, scale), (query, keys, values)
    )
    back = lax.all_to_all(
        attended.reshape(seq_count, length, 1, local_heads * HD),
        "seq",
        split_axis=1,
        concat_axis=2,
        tiled=True,
    )
    attn_out = back.reshape(rows, width)
    hidden = inputs + jnp.dot(attn_out, proj_out, preferred_element_type=jnp.float32)
    normed_two, inverse_two = normalize(hidden)
    ffn_in = (normed_two * gain_two.astype(jnp.float32)).astype(jnp.bfloat16)
    gate_up = jnp.dot(ffn_in, proj_in, preferred_element_type=jnp.float32)
    gate_part, up_part = (gate_up[:, :FF], gate_up[:, FF:])
    activated, gelu_back = jax.vjp(exact_gelu, gate_part)
    product = (activated * up_part).astype(jnp.bfloat16)
    output = hidden + jnp.dot(product, proj_down, preferred_element_type=jnp.float32)
    result = output.astype(jnp.bfloat16).reshape(seq_count, tokens_dev, width)
    grad_output = cotangent.reshape(rows, width)
    grad_down = contract_rows(product, grad_output)
    grad_product = times_transpose(grad_output, proj_down)
    grad_gate = gelu_back(grad_product * up_part)[0]
    grad_mixed_ffn = jnp.concatenate([grad_gate, grad_product * activated], axis=1).astype(
        jnp.bfloat16
    )
    grad_in = contract_rows(ffn_in, grad_mixed_ffn)
    grad_normed_two = times_transpose(grad_mixed_ffn, proj_in)
    grad_gain_two = jnp.sum(grad_normed_two * normed_two, axis=0)
    grad_hidden = grad_output.astype(jnp.float32) + norm_back(
        grad_normed_two, normed_two, inverse_two, gain_two.astype(jnp.float32)
    )
    grad_branch = grad_hidden.astype(jnp.bfloat16)
    grad_proj_out = contract_rows(attn_out, grad_branch)
    grad_attn = times_transpose(grad_branch, proj_out).astype(jnp.bfloat16)
    grad_heads = lax.all_to_all(
        grad_attn.reshape(seq_count, tokens_dev, parts, local_heads * HD),
        "seq",
        split_axis=2,
        concat_axis=1,
        tiled=True,
    )
    grad_heads = grad_heads.reshape(seq_count, length, local_heads, HD)
    grad_query, grad_keys, grad_values = lax.map(
        lambda item: attend_back(item[0], item[1], item[2], item[3], item[4], block, scale),
        (query, keys, values, grad_heads, logsum),
    )
    grad_stack = jnp.stack([grad_query, grad_keys, grad_values], axis=2).reshape(
        seq_count, length, 3, 1, local_heads * HD
    )
    grad_tokens = lax.all_to_all(grad_stack, "seq", split_axis=1, concat_axis=3, tiled=True)
    grad_tokens = grad_tokens.reshape(seq_count, tokens_dev, 3, H, HD).astype(jnp.float32)
    grad_raw = (
        jnp.stack(
            [
                rotate_back(grad_tokens[:, :, 0], cosine, sine),
                rotate_back(grad_tokens[:, :, 1], cosine, sine),
                grad_tokens[:, :, 2],
            ],
            axis=2,
        )
        .reshape(rows, 3 * width)
        .astype(jnp.bfloat16)
    )
    grad_proj_qkv = contract_rows(attn_in, grad_raw)
    grad_normed_one = times_transpose(grad_raw, proj_qkv)
    grad_gain_one = jnp.sum(grad_normed_one * normed_one, axis=0)
    grad_inputs = grad_hidden + norm_back(
        grad_normed_one, normed_one, inverse_one, gain_one.astype(jnp.float32)
    )
    shares = (
        lax.psum_scatter(grad_gain_one, "dp", scatter_dimension=0, tiled=True),
        lax.psum_scatter(grad_proj_qkv, "dp", scatter_dimension=0, tiled=True),
        lax.psum_scatter(grad_proj_out, "dp", scatter_dimension=0, tiled=True),
        lax.psum_scatter(grad_gain_two, "dp", scatter_dimension=0, tiled=True),
        lax.psum_scatter(grad_in, "dp", scatter_dimension=0, tiled=True),
        lax.psum_scatter(grad_down, "dp", scatter_dimension=1, tiled=True),
    )
    totals = (
        lax.psum(shares[0].astype(jnp.bfloat16), "seq").astype(jnp.float32),
        lax.psum(shares[1].astype(jnp.bfloat16), "seq").astype(jnp.float32),
        lax.psum(shares[2].astype(jnp.bfloat16), "seq").astype(jnp.float32),
        lax.psum(shares[3].astype(jnp.bfloat16), "seq").astype(jnp.float32),
        lax.psum(shares[4].astype(jnp.bfloat16), "seq").astype(jnp.float32),
        lax.psum(shares[5].astype(jnp.bfloat16), "seq").astype(jnp.float32),
    )
    return (
        result,
        grad_inputs.reshape(seq_count, tokens_dev, width),
        totals[0],
        totals[1],
        totals[2],
        totals[3],
        totals[4],
        totals[5],
    )


def solution(mesh):
    in_specs = (
        P("dp", "seq", None),
        P("dp", "seq", None),
        P("dp"),
        P("dp", None),
        P("dp", None),
        P("dp"),
        P("dp", None),
        P(None, "dp"),
    )
    out_specs = (
        P("dp", "seq", None),
        P("dp", "seq", None),
        P("dp"),
        P("dp", None),
        P("dp", None),
        P("dp"),
        P("dp", None),
        P(None, "dp"),
    )
    return jax.shard_map(shards, mesh=mesh, in_specs=in_specs, out_specs=out_specs, check_vma=False)
```

profile of v0, /device:TPU:1, one launch (start us, length us, event | category | flops | bytes accessed | tf_op | source)
XLA Modules:
  0.0 986.2 jit_solution(8106195189040218216)
XLA Ops:
  11.6 19.6 %all-reduce.5 = (bf16[768]{0:T(1024)(128)(2,1)S(1)}, bf16[768]{0:T(1024)(128)(2,1)}) all-reduce(bf16[768]{0:T(1024)(128)(2,1)S(1)} %dynamic-update-slice, bf16[768]{0:T(1024)(128)(2,1)S(1)} %dynamic-update-slice.1), channel_id=1, replica_groups=mesh['dp'=8,'seq'=4] {'dp'}, use_global_device_ids=true, to_apply=%add | all-reduce | flops 1536 | bytes 6144
  37.5 39.2 %all-gather.5.cloned.1.call-done = bf16[768,2304]{1,0:T(8,128)(2,1)} async-done(((bf16[96,2304]{1,0:T(8,128)(2,1)}), bf16[768,2304]{1,0:T(8,128)(2,1)}) %all-gather.5.cloned.1.call-update) | async-done | bytes 3538960 | tf_op jit(solution)/shard_map/all_gather | solution.py:137
  102.6 51.5 %all-to-all-done = bf16[2,512,3,4,192]{1,4,0,2,3:T(8,128)(2,1)} async-done(((bf16[2,512,3,4,192]{1,4,0,2,3:T(8,128)(2,1)}), bf16[2,512,3,4,192]{1,4,0,2,3:T(8,128)(2,1)}, u32[]{:S(2)}, u32[]{:S(2)}) %all-to-all-start) | async-done | bytes 4718624 | tf_op jit(solution)/shard_map/all_to_all | solution.py:161
  177.1 78.4 %while.54 = (s32[]{:T(128)}, bf16[2,2048,3,64]{1,3,2,0:T(8,128)(2,1)}, f32[2,4,3,512]{3,2,1,0:T(4,128)S(1)}, bf16[2,2048,3,64]{1,3,2,0:T(8,128)(2,1)}, bf16[2,20...) while((s32[]{:T(128)}, ...), condition=%wide.region_7.8_spmd, body=%wide.region_2.7_spmd.sunk | while | flops 833714688 | bytes 55568688 | solution.py:164
  181.4 31.4 %while.57 = (s32[]{:T(128)}, bf16[4,512,3,64]{1,3,2,0:T(8,128)(2,1)S(1)}, f32[4,3,512]{2,1,0:T(4,128)S(1)}, bf16[4,512,3,64]{1,3,2,0:T(8,128)(2,1)S(1)}, bf16[20...) while((s32[]{:T(128)}, bf16[4,512,3,64]{1,3,2,0:T(8,128)(2,1)S(1)}, ...), condition=%wide.region_6.6_spmd, body=%wide.region_3.5_spmd.sunk | while | flops 833714688 | bytes 42920060 | solution.py:78
  220.6 31.4 %while.57 = (s32[]{:T(128)}, bf16[4,512,3,64]{1,3,2,0:T(8,128)(2,1)S(1)}, f32[4,3,512]{2,1,0:T(4,128)S(1)}, bf16[4,512,3,64]{1,3,2,0:T(8,128)(2,1)S(1)}, bf16[20...) while((s32[]{:T(128)}, bf16[4,512,3,64]{1,3,2,0:T(8,128)(2,1)S(1)}, ...), condition=%wide.region_6.6_spmd, body=%wide.region_3.5_spmd.sunk | while | flops 833714688 | bytes 42920060 | solution.py:78
  267.0 23.8 %all-to-all-done.1 = bf16[2,2048,1,192]{3,0,2,1:T(2,128)(2,1)S(1)} async-done(((bf16[2,2048,1,192]{3,0,2,1:T(2,128)(2,1)}), bf16[2,2048,1,192]{3,0,2,1:T(2,128)(2,1)S(1)}, u32[]{:S(2)}, u32[]{:S(2)}) %all-to-all-start.1) | async-done | bytes 1572896 | tf_op jit(solution)/shard_map/all_to_all | solution.py:167
  292.1 9.4 copy.83
  308.7 10.7 %fusion.82 = f32[1024,2304]{1,0:T(8,128)} fusion(bf16[768,2304]{1,0:T(8,128)(2,1)} %all-gather.9.cloned.1.call-done, f32[1024,768]{1,0:T(8,128)} %copy-done.7, f32[768]{0:T(1024)S(1)} %convert_element_type.156, f32[1024]{0:T(1024)S(1)} %add_rsqrt_fusion, f32[1024]{0:T(1024)S(1)} %broadcast_multiply_fusion.5), kind=kOutput, calls=%fused_computation.167 | convolution fusion | flops 3627024384 | bytes 16133120 | tf_op jit(solution)/shard_map/dot_general | solution.py:178
  319.4 16.2 %add_convert_fusion = (bf16[1024,1152]{1,0:T(8,128)(2,1)}, f32[1024,1152]{1,0:T(8,128)S(1)}, f32[1024,1152]{1,0:T(8,128)S(1)}) fusion(f32[1024,2304]{1,0:T(8,128)} %fusion.82, bf16[1024,768]{1,0:T(8,128)(2,1)S(1)} %bitcast.289, bf16[1152,768]{0,1:T(8,128)(2,1)} %all-gather.11.cloned.1.call-done), kind=kOutput, calls=%fused_computation.65 | convolution fusion | flops 1898053632 | bytes 24576000 | tf_op jit(solution)/shard_map/dot_general | solution.py:60
  375.7 9.5 fusion.65
  385.3 9.8 all-to-all-done.2
  404.3 236.6 %while.56 = (s32[]{:T(128)}, bf16[2,2048,3,64]{1,3,2,0:T(8,128)(2,1)}, bf16[2,2048,3,64]{1,3,2,0:T(8,128)(2,1)}, bf16[2,2048,3,64]{1,3,2,0:T(8,128)(2,1)}, bf16[...) while((s32[]{:T(128)}, ...), condition=%wide.region_16.17_spmd, body=%wide.region_12.16_spmd.sunk | while | flops 2053863936 | bytes 164456976 | solution.py:208
  411.4 99.5 %while.58 = (s32[]{:T(128)}, f32[2048,3,64]{0,2,1:T(8,128)}, f32[2048,3,64]{0,2,1:T(8,128)S(1)}, bf16[4,512,3,64]{1,3,2,0:T(8,128)(2,1)}, bf16[4,512,3,64]{1,3,2...) while((s32[]{:T(128)}, f32[2048,3,64]{0,2,1:T(8,128)}, ...), condition=%wide.region_15.15_spmd.clone, body=%wide.region_13.14_spmd.clone.sunk | while | flops 2053077504 | bytes 129411248 | solution.py:119
  529.7 99.7 %while.58 = (s32[]{:T(128)}, f32[2048,3,64]{0,2,1:T(8,128)}, f32[2048,3,64]{0,2,1:T(8,128)S(1)}, bf16[4,512,3,64]{1,3,2,0:T(8,128)(2,1)}, bf16[4,512,3,64]{1,3,2...) while((s32[]{:T(128)}, f32[2048,3,64]{0,2,1:T(8,128)}, ...), condition=%wide.region_15.15_spmd.clone, body=%wide.region_13.14_spmd.clone.sunk | while | flops 2053077504 | bytes 129411248 | solution.py:119
  646.0 16.3 %copy.89 = bf16[2,2048,3,1,192]{4,0,3,2,1:T(2,128)(2,1)} copy(bf16[2,2048,3,1,192]{1,4,0,3,2:T(8,128)(2,1)} %pad_maximum_fusion.2) | data formatting | bytes 9437184 | tf_op jit(solution)/shard_map/stack | solution.py:212
  662.3 77.3 %all_to_all.54 = bf16[2,2048,3,1,192]{4,0,3,2,1:T(2,128)(2,1)} all-to-all(bf16[2,2048,3,1,192]{4,0,3,2,1:T(2,128)(2,1)} %copy.89), channel_id=1, replica_groups=mesh['dp'=8,'seq'=4] {'seq'}, dimensions={1} | all-to-all | bytes 9437184 | tf_op jit(solution)/shard_map/all_to_all | solution.py:215
  739.6 15.8 %copy.90 = bf16[2,2048,3,1,192]{1,4,3,2,0:T(8,128)(2,1)} copy(bf16[2,2048,3,1,192]{4,0,3,2,1:T(2,128)(2,1)} %all_to_all.54) | data formatting | bytes 9437184 | tf_op jit(solution)/shard_map/all_to_all | solution.py:215
  755.4 11.9 %reshape.358 = f32[2,4,512,3,1,192]{2,1,5,3,0,4:T(4,128)} reshape(bf16[2,2048,3,1,192]{1,4,3,2,0:T(8,128)(2,1)} %copy.90) | data formatting | bytes 14155776 | tf_op jit(solution)/shard_map/convert_element_type | solution.py:216
  780.8 9.4 copy.92
  816.2 17.7 %all-reduce.4 = (bf16[768]{0:T(1024)(128)(2,1)S(1)}, bf16[768]{0:T(1024)(128)(2,1)S(1)}) all-reduce(f32[768]{0:T(1024)S(1)} %get-tuple-element.290, f32[768]{0:T(1024)S(1)} %copy-done.29), channel_id=2, replica_groups=mesh['dp'=8,'seq'=4] {'dp'}, use_global_device_ids=true, to_apply=%region_20.21.clone | all-reduce | flops 1536 | bytes 9216
  834.1 9.9 %all-reduce.6 = (bf16[96]{0:T(256)(128)(2,1)S(1)}, bf16[96]{0:T(256)(128)(2,1)S(1)}) all-reduce(bf16[96]{0:T(256)(128)(2,1)S(1)} %dynamic-slice.9, bf16[96]{0:T(256)(128)(2,1)S(1)} %dynamic-slice.8), channel_id=1, replica_groups=mesh['dp'=8,'seq'=4] {'seq'}, use_global_device_ids=true, to_apply=%region_21.22 | all-reduce | flops 192 | bytes 768 | tf_op jit(solution)/shard_map/psum | solution.py:244
  850.4 79.4 %reduce-scatter.5.cloned.1.call-done = f32[96,2304]{1,0:T(8,128)} async-done(((f32[768,2304]{1,0:T(8,128)}), f32[96,2304]{1,0:T(8,128)}) %reduce-scatter.5.cloned.1.call-update) | async-done | bytes 884752 | tf_op jit(solution)/shard_map/reduce_scatter | solution.py:237
  936.4 35.7 %all-reduce.10.cloned.1.call-done = (bf16[96,2304]{1,0:T(8,128)(2,1)}, bf16[96,768]{1,0:T(8,128)(2,1)}, bf16[96,2304]{1,0:T(8,128)(2,1)}, bf16[1152,96]{0,1:T(8,128)(2,1)}) async-done(((bf16[96,2304]{1,0:T(8,128)(2,1)}, bf16[96,768]{1,0:T(8,128)(2,1)}, bf16[96,2304]{1,0:T(8,128)(2,1)}, bf16[1152,96]{0,1:T(8,128)(2,1)}), (bf16[96,2304]{1,0:T(8,128)(2,1)}, bf16[96,768]{1,0:T(8,128)(2,1)}, ...) | async-done | bytes 1253392 | tf_op jit(solution)/shard_map/psum | solution.py:245
  (354 shorter events, 506.6 us)
Async XLA Ops:
  7.2 27.4 %copy-start.2 = (bf16[2,512,768]{2,1,0:T(8,128)(2,1)S(1)}, bf16[2,512,768]{2,1,0:T(8,128)(2,1)}, u32[]{:S(2)}) copy-start(bf16[2,512,768]{2,1,0:T(8,128)(2,1)} %param.16) | copy-start | bytes 4718596
  7.2 69.5 %all-gather.5.cloned.1.call-start = ((), (), s32[]{:S(2)}) async-start(), calls=%async_computation.8 | async-start | bytes 3981312 | tf_op jit(solution)/shard_map/all_gather | solution.py:137
  94.6 59.6 %all-to-all-start = ((bf16[2,512,3,4,192]{1,4,0,2,3:T(8,128)(2,1)}), bf16[2,512,3,4,192]{1,4,0,2,3:T(8,128)(2,1)}, u32[]{:S(2)}, u32[]{:S(2)}) async-start(bf16[2,512,3,4,192]{1,4,0,2,3:T(8,128)(2,1)} %copy.94), calls=%async_computation | async-start | bytes 9437184 | tf_op jit(solution)/shard_map/all_to_all | solution.py:161
  101.2 201.9 %all-gather.7.cloned.1.call-start = ((), (), s32[]{:S(2)}) async-start(), calls=%async_computation.9 | async-start | bytes 1327104 | tf_op jit(solution)/shard_map/all_gather | solution.py:138
  101.9 206.8 %all-gather.9.cloned.1.call-start = ((), (), s32[]{:S(2)}) async-start(), calls=%async_computation.10 | async-start | bytes 3981312 | tf_op jit(solution)/shard_map/all_gather | solution.py:140
  255.4 11.5 %copy-start.30 = (bf16[768]{0:T(1024)(128)(2,1)S(1)}, bf16[768]{0:T(1024)(128)(2,1)}, u32[]{:S(2)}) copy-start(bf16[768]{0:T(1024)(128)(2,1)} %get-tuple-element.357) | copy-start | bytes 4612
  261.5 29.3 %all-to-all-start.1 = ((bf16[2,2048,1,192]{3,0,2,1:T(2,128)(2,1)}), bf16[2,2048,1,192]{3,0,2,1:T(2,128)(2,1)S(1)}, u32[]{:S(2)}, u32[]{:S(2)}) async-start(bf16[2,2048,1,192]{3,0,2,1:T(2,128)(2,1)} %copy.82), calls=%async_computation.1 | async-start | bytes 4194304 | tf_op jit(solution)/shard_map/all_to_all | solution.py:167
  266.0 53.5 %all-gather.11.cloned.1.call-start = ((), (), s32[]{:S(2)}) async-start(), calls=%async_computation.11 | async-start | bytes 1990656 | tf_op jit(solution)/shard_map/all_gather | solution.py:141
  266.5 578.6 %reduce-scatter.7.cloned.1.call-start = ((), (), s32[]{:S(2)}) async-start(), calls=%async_computation.13 | async-start | bytes 2654208 | tf_op jit(solution)/shard_map/reduce_scatter | solution.py:238
  292.1 11.0 %copy-start.3 = (bf16[2,512,768]{2,1,0:T(8,128)(2,1)S(1)}, bf16[2,512,768]{2,1,0:T(8,128)(2,1)}, u32[]{:S(2)}) copy-start(bf16[2,512,768]{2,1,0:T(8,128)(2,1)} %param.16) | copy-start | bytes 4718596
  308.7 10.7 %copy-start.15 = (bf16[2,512,768]{2,1,0:T(8,128)(2,1)S(1)}, bf16[2,512,768]{2,1,0:T(8,128)(2,1)}, u32[]{:S(2)}) copy-start(bf16[2,512,768]{2,1,0:T(8,128)(2,1)} %param.17) | copy-start | bytes 4718596
  319.4 16.2 %slice-start = ((s8[9437184]{0:T(1024)(128)(4,1)}), s8[4194304]{0:T(1024)(128)(4,1)S(1)}, s32[]{:S(2)}) async-start(s8[9437184]{0:T(1024)(128)(4,1)} %bitcast.272), calls=%async_computation.17 | async-start | bytes 8388608
  319.4 16.2 %slice-start.1 = ((s8[9437184]{0:T(1024)(128)(4,1)}), s8[4194304]{0:T(1024)(128)(4,1)S(1)}, s32[]{:S(2)}) async-start(s8[9437184]{0:T(1024)(128)(4,1)} %bitcast.272), calls=%async_computation.18 | async-start | bytes 8388608
  319.4 16.2 %slice-start.2 = ((s8[9437184]{0:T(1024)(128)(4,1)}), s8[1048576]{0:T(1024)(128)(4,1)S(1)}, s32[]{:S(2)}) async-start(s8[9437184]{0:T(1024)(128)(4,1)} %bitcast.272), calls=%async_computation.19 | async-start | bytes 2097152
  338.1 9.0 copy-start.14
  340.3 6.7 copy-start.16
  353.0 493.7 %reduce-scatter.11.cloned.1.call-start = ((), (), s32[]{:S(2)}) async-start(), calls=%async_computation.15 | async-start | bytes 3981312 | tf_op jit(solution)/shard_map/reduce_scatter | solution.py:241
  370.5 24.5 %all-to-all-start.2 = ((bf16[2,512,4,192]{1,0,3,2:T(2,128)(2,1)}), bf16[2,512,4,192]{1,0,3,2:T(2,128)(2,1)}, u32[]{:S(2)}, u32[]{:S(2)}) async-start(bf16[2,512,4,192]{1,0,3,2:T(2,128)(2,1)} %reshape.353), calls=%async_computation.2 | async-start | bytes 3145728 | tf_op jit(solution)/shard_map/all_to_all | solution.py:200
  375.7 472.7 %reduce-scatter.9.cloned.1.call-start = ((), (), s32[]{:S(2)}) async-start(), calls=%async_computation.14 | async-start | bytes 7962624 | tf_op jit(solution)/shard_map/reduce_scatter | solution.py:240
  385.2 544.6 %reduce-scatter.5.cloned.1.call-start = ((), (), s32[]{:S(2)}) async-start(), calls=%async_computation.12 | async-start | bytes 7962624 | tf_op jit(solution)/shard_map/reduce_scatter | solution.py:237
  511.0 10.3 %copy-start.1 = (f32[2048,3,64]{0,2,1:T(8,128)S(1)}, f32[2048,3,64]{0,2,1:T(8,128)}, u32[]{:S(2)}) copy-start(f32[2048,3,64]{0,2,1:T(8,128)} %get-tuple-element.628) | copy-start | bytes 4718596 | tf_op jit(solution)/shard_map/while
  629.3 10.2 %copy-start.1 = (f32[2048,3,64]{0,2,1:T(8,128)S(1)}, f32[2048,3,64]{0,2,1:T(8,128)}, u32[]{:S(2)}) copy-start(f32[2048,3,64]{0,2,1:T(8,128)} %get-tuple-element.628) | copy-start | bytes 4718596 | tf_op jit(solution)/shard_map/while
  767.3 6.7 copy-start.22
  802.3 169.8 %all-reduce.10.cloned.1.call-start = ((), (), s32[]{:S(2)}) async-start(), calls=%async_computation.16 | async-start | bytes 2506752 | tf_op jit(solution)/shard_map/psum | solution.py:245
  (42 other events, 150.9 us)
Sparse Core Ops, SparseCore 0:
  10.2 66.4 all-gather.4
  104.2 38.4 all-gather.6
  144.8 64.0 all-gather.8
  268.6 43.6 all-gather.10
  353.1 66.5 reduce-scatter.6
  423.2 79.0 reduce-scatter.10
  506.0 127.8 reduce-scatter.8
  802.4 127.3 reduce-scatter.4
  933.1 39.0 all-reduce.9
where the time goes:
time: 998 us; the launch traced here: 986 us
  matrix products  289 us (29%)
  waiting for transfers between devices  242 us (24%)
  local copies, waits for them, and re-layouts  191 us (19%)
  blocking collectives  125 us (13%)
  other arithmetic  106 us (11%)
  starting transfers between devices  17.3 us (2%)
  between operations  15.8 us (2%)
    reduce_scatter x1, waiting for transfers between devices, shards(): lax.psum_scatter(grad_proj_qkv, 'dp', scatter_dimension=0, tiled=True)  79.4 us
    all_to_all x1, blocking collectives, shards(): lax.all_to_all(grad_stack, 'seq', split_axis=1, concat_axis=3, tiled=True)  77.3 us
    all_to_all x1, waiting for transfers between devices, shards(): lax.all_to_all(sending, 'seq', split_axis=3, concat_axis=1, tiled=True)  51.5 us
    dot_general x8, matrix products, one_block(): jnp.einsum('hqk,khd->qhd', grad_scores, keys, preferred_element_type=jnp....  45.4 us
    all_gather x1, waiting for transfers between devices, shards(): lax.all_gather(w_qkv, 'dp', axis=0, tiled=True)  39.2 us
    dot_general x16, matrix products, one_block(): jnp.einsum('qhd,khd->hqk', rows, keys, preferred_element_type=jnp.float32)  37.5 us
    unnamed x2, blocking collectives  37.3 us
    convert_element_type x8, other arithmetic, one_block(): grad_scores = (probs * (grad_probs - inner)).astype(jnp.bfloat16)  36.9 us
  transfers between devices with their start and end apart: 12, of which 6 were waited for; matrix products, arithmetic and copies ran while one was open for 53% of the time, Pallas kernels for 0%

commit v1 on v0

v1 whole, which is shorter than its diff:
```python
import functools
import math

import jax
import jax.numpy as jnp
from jax import lax
from jax.experimental import pallas as pl
from jax.experimental.pallas import tpu as pltpu
from jax.sharding import PartitionSpec as P

H = 12
HD = 64
FF = 1152


rope_base = 160000.0
norm_eps = 1e-05


def normalize(values):
    centre = values - jnp.mean(values, axis=-1, keepdims=True)
    inverse = lax.rsqrt(jnp.mean(centre * centre, axis=-1, keepdims=True) + norm_eps)
    return (centre * inverse, inverse)


def norm_back(grad_normed, normed, inverse, gain):
    scaled = grad_normed * gain
    first = jnp.mean(scaled, axis=-1, keepdims=True)
    second = jnp.mean(scaled * normed, axis=-1, keepdims=True)
    return inverse * (scaled - first - normed * second)


def rope_tables(positions):
    half = HD // 2
    freqs = rope_base ** (-(jnp.arange(half, dtype=jnp.float32) * 2.0) / HD)
    angles = positions.astype(jnp.float32)[:, None] * freqs[None, :]
    angles = jnp.concatenate([angles, angles], axis=-1)
    return (jnp.cos(angles), jnp.sin(angles))


def rotate(values, cosine, sine):
    half = values.shape[-1] // 2
    turned = jnp.concatenate([-values[..., half:], values[..., :half]], axis=-1)
    return values * cosine[:, None, :] + turned * sine[:, None, :]


def rotate_back(grads, cosine, sine):
    half = grads.shape[-1] // 2
    moved = grads * sine[:, None, :]
    turned = jnp.concatenate([moved[..., half:], -moved[..., :half]], axis=-1)
    return grads * cosine[:, None, :] + turned


def exact_gelu(values):
    return jax.nn.gelu(values, approximate=False)


def contract_rows(left, right):
    return lax.dot_general(
        left, right, (((0,), (0,)), ((), ())), preferred_element_type=jnp.float32
    )


def times_transpose(left, right):
    return lax.dot_general(
        left, right, (((1,), (1,)), ((), ())), preferred_element_type=jnp.float32
    )


SCALE = HD ** (-0.5)
TO_BASE2 = SCALE * math.log2(math.e)
VMEM_LIMIT = 56 * 1024 * 1024


def dot_nt(left, right):
    return lax.dot_general(
        left, right, (((1,), (1,)), ((), ())), preferred_element_type=jnp.float32
    )


def dot_nn(left, right):
    return lax.dot_general(
        left, right, (((1,), (0,)), ((), ())), preferred_element_type=jnp.float32
    )


def only_head(values, head):
    lanes = lax.broadcasted_iota(jnp.int32, values.shape, 1)
    mine = (lanes < HD) if head == 0 else (lanes >= HD)
    return jnp.where(mine, values, jnp.zeros_like(values))


def join_heads(first, second):
    lanes = lax.broadcasted_iota(jnp.int32, first.shape, 1)
    return jnp.where(lanes < HD, first, second)


def attend_kernel(q_ref, k_ref, v_ref, out_ref, lse_ref, wide_ref):
    @pl.when(pl.program_id(1) == 0)
    def _():
        wide_ref[:, : 2 * HD] = v_ref[...]
        wide_ref[:, 2 * HD :] = jnp.ones_like(v_ref)

    outs, sums = [], []
    for head in range(2):
        scores = dot_nt(only_head(q_ref[...], head), k_ref[...])
        top = jnp.max(scores, axis=-1, keepdims=True)
        weights = jnp.exp2((scores - top) * TO_BASE2).astype(jnp.bfloat16)
        both = dot_nn(weights, wide_ref[...])
        total = both[:, 2 * HD :]
        outs.append(both[:, : 2 * HD] / total)
        sums.append(top * TO_BASE2 + jnp.log2(total))
    out_ref[...] = join_heads(outs[0], outs[1]).astype(jnp.bfloat16)
    turned = join_heads(sums[0], sums[1]).T
    lse_ref[0, 0:1, :] = turned[0:1]
    lse_ref[0, 1:2, :] = turned[HD : HD + 1]


def attend(query, keys, values, block):
    rows, width = query.shape
    length = keys.shape[0]
    pairs = width // (2 * HD)
    return pl.pallas_call(
        attend_kernel,
        grid=(pairs, rows // block),
        in_specs=[
            pl.BlockSpec((block, 2 * HD), lambda p, i: (i, p)),
            pl.BlockSpec((length, 2 * HD), lambda p, i: (0, p)),
            pl.BlockSpec((length, 2 * HD), lambda p, i: (0, p + pairs)),
        ],
        out_specs=[
            pl.BlockSpec((block, 2 * HD), lambda p, i: (i, p)),
            pl.BlockSpec((1, 8, block), lambda p, i: (p, 0, i)),
        ],
        out_shape=[
            jax.ShapeDtypeStruct((rows, width), jnp.bfloat16),
            jax.ShapeDtypeStruct((pairs, 8, rows), jnp.float32),
        ],
        scratch_shapes=[pltpu.VMEM((length, 4 * HD), jnp.bfloat16)],
        compiler_params=pltpu.CompilerParams(vmem_limit_bytes=VMEM_LIMIT),
        cost_estimate=pl.CostEstimate(
            flops=16 * rows * length * width,
            bytes_accessed=4 * length * width + 4 * rows * width,
            transcendentals=rows * length * width // HD,
        ),
        name="attend",
    )(query, keys, values)


def attend_back_kernel(
    q_ref, do_ref, o_ref, lse_ref, k_ref, v_ref, dq_ref, dk_ref, dv_ref, acc_ref, delta_ref
):
    step = pl.program_id(1)

    @pl.when(step == 0)
    def _():
        both = (do_ref[...].astype(jnp.float32) * o_ref[...].astype(jnp.float32)).T
        delta_ref[0:1, :] = jnp.sum(both[:HD], axis=0, keepdims=True)
        delta_ref[1:2, :] = jnp.sum(both[HD:], axis=0, keepdims=True)
        acc_ref[...] = jnp.zeros_like(acc_ref)

    keys = k_ref[...]
    turned_keys = keys.astype(jnp.float32).T.astype(jnp.bfloat16)
    grad_keys, grad_values = [], []
    for head in range(2):
        scores = dot_nt(keys, only_head(q_ref[...], head))
        probs = jnp.exp2(scores * TO_BASE2 - lse_ref[0, head : head + 1, :])
        grad_probs = dot_nt(v_ref[...], only_head(do_ref[...], head))
        grad_scores = (probs * (grad_probs - delta_ref[head : head + 1, :])).astype(jnp.bfloat16)
        grad_values.append(dot_nn(probs.astype(jnp.bfloat16), do_ref[...]))
        grad_keys.append(dot_nn(grad_scores, q_ref[...]))
        acc_ref[head * HD : (head + 1) * HD, :] += dot_nn(
            turned_keys[head * HD : (head + 1) * HD], grad_scores
        )
    dv_ref[...] = join_heads(grad_values[0], grad_values[1]).astype(jnp.bfloat16)
    dk_ref[...] = (join_heads(grad_keys[0], grad_keys[1]) * SCALE).astype(jnp.bfloat16)

    @pl.when(step == pl.num_programs(1) - 1)
    def _():
        dq_ref[...] = (acc_ref[...].T * SCALE).astype(jnp.bfloat16)


def attend_back(query, grads, outs, lse, keys, block):
    rows, width = query.shape
    length = keys.shape[0]
    pairs = width // (2 * HD)
    own = pl.BlockSpec((rows, 2 * HD), lambda p, i: (0, p))
    return pl.pallas_call(
        attend_back_kernel,
        grid=(pairs, length // block),
        in_specs=[
            own,
            own,
            own,
            pl.BlockSpec((1, 8, rows), lambda p, i: (p, 0, 0)),
            pl.BlockSpec((block, 2 * HD), lambda p, i: (i, p)),
            pl.BlockSpec((block, 2 * HD), lambda p, i: (i, p + pairs)),
        ],
        out_specs=[
            own,
            pl.BlockSpec((block, 2 * HD), lambda p, i: (i, p)),
            pl.BlockSpec((block, 2 * HD), lambda p, i: (i, p)),
        ],
        out_shape=[
            jax.ShapeDtypeStruct((rows, width), jnp.bfloat16),
            jax.ShapeDtypeStruct((length, width), jnp.bfloat16),
            jax.ShapeDtypeStruct((length, width), jnp.bfloat16),
        ],
        scratch_shapes=[
            pltpu.VMEM((2 * HD, rows), jnp.float32),
            pltpu.VMEM((8, rows), jnp.float32),
        ],
        compiler_params=pltpu.CompilerParams(vmem_limit_bytes=VMEM_LIMIT),
        cost_estimate=pl.CostEstimate(
            flops=40 * rows * length * width,
            bytes_accessed=8 * length * width + 8 * rows * width,
            transcendentals=rows * length * width // HD,
        ),
        name="attend_back",
    )(query, grads, outs, lse, keys, keys)


def gelu_parts(values):
    cdf = 0.5 + 0.5 * lax.erf(values * (0.5**0.5))
    slope = cdf + values * ((2.0 * math.pi) ** -0.5) * jnp.exp(-0.5 * values * values)
    return (values * cdf, slope)


def half_turn(chunk):
    lanes = lax.broadcasted_iota(jnp.int32, chunk.shape, 1)
    half = HD // 2
    ahead = pltpu.roll(chunk, chunk.shape[1] - half, axis=1)
    behind = pltpu.roll(chunk, half, axis=1)
    return jnp.where(lanes % HD < half, ahead, behind)


def project_kernel(x_ref, gain_ref, w_ref, cos_ref, sin_ref, in_ref, q_ref, kv_ref):
    normed, _ = normalize(x_ref[...].astype(jnp.float32))
    attn_in = (normed * gain_ref[...]).astype(jnp.bfloat16)
    in_ref[...] = attn_in
    width = x_ref.shape[1]
    cosine, sine = cos_ref[...], sin_ref[...]
    for part, target, start in ((0, q_ref, 0), (1, kv_ref, 0), (2, kv_ref, width)):
        mixed = dot_nn(attn_in, w_ref[:, part * width : (part + 1) * width])
        for at in range(0, width, 2 * HD):
            chunk = mixed[:, at : at + 2 * HD]
            if part < 2:
                chunk = chunk * cosine + half_turn(chunk) * sine
            target[:, start + at : start + at + 2 * HD] = chunk.astype(jnp.bfloat16)


def project(inputs, gain, weights, cosine, sine, block):
    rows, width = inputs.shape
    by_rows = lambda columns: pl.BlockSpec((block, columns), lambda i: (i, 0))
    whole = lambda array: pl.BlockSpec(array.shape, lambda i: (0, 0))
    return pl.pallas_call(
        project_kernel,
        grid=(rows // block,),
        in_specs=[
            by_rows(width),
            whole(gain),
            whole(weights),
            by_rows(2 * HD),
            by_rows(2 * HD),
        ],
        out_specs=[by_rows(width), by_rows(width), by_rows(2 * width)],
        out_shape=[
            jax.ShapeDtypeStruct((rows, width), jnp.bfloat16),
            jax.ShapeDtypeStruct((rows, width), jnp.bfloat16),
            jax.ShapeDtypeStruct((rows, 2 * width), jnp.bfloat16),
        ],
        compiler_params=pltpu.CompilerParams(vmem_limit_bytes=VMEM_LIMIT),
        cost_estimate=pl.CostEstimate(
            flops=6 * rows * width * width, bytes_accessed=14 * rows * width, transcendentals=0
        ),
        name="project",
    )(inputs, gain, weights, cosine, sine)


def feed_kernel(
    x_ref, attn_ref, g_ref, gain_ref, wo_ref, wi_ref, wd_ref,
    out_ref, fin_ref, prod_ref, gmix_ref, ghid_ref, gbr_ref, gattn_ref, ggain_ref,
):
    @pl.when(pl.program_id(0) == 0)
    def _():
        ggain_ref[...] = jnp.zeros_like(ggain_ref)

    gain = gain_ref[...]
    hidden = x_ref[...].astype(jnp.float32) + dot_nn(attn_ref[...], wo_ref[...])
    normed, inverse = normalize(hidden)
    ffn_in = (normed * gain).astype(jnp.bfloat16)
    fin_ref[...] = ffn_in
    grads = g_ref[...]
    gate_part = dot_nn(ffn_in, wi_ref[:, :FF])
    up_part = dot_nn(ffn_in, wi_ref[:, FF:])
    activated, slope = gelu_parts(gate_part)
    product = (activated * up_part).astype(jnp.bfloat16)
    prod_ref[...] = product
    out_ref[...] = (hidden + dot_nt(product, wd_ref[...])).astype(jnp.bfloat16)
    grad_product = dot_nn(grads, wd_ref[...])
    grad_gate = (grad_product * up_part * slope).astype(jnp.bfloat16)
    grad_up = (grad_product * activated).astype(jnp.bfloat16)
    gmix_ref[:, :FF] = grad_gate
    gmix_ref[:, FF:] = grad_up
    grad_normed = dot_nt(grad_gate, wi_ref[:, :FF]) + dot_nt(grad_up, wi_ref[:, FF:])
    ggain_ref[0:1, :] += jnp.sum(grad_normed * normed, axis=0, keepdims=True)
    grad_hidden = grads.astype(jnp.float32) + norm_back(grad_normed, normed, inverse, gain)
    ghid_ref[...] = grad_hidden
    branch = grad_hidden.astype(jnp.bfloat16)
    gbr_ref[...] = branch
    gattn_ref[...] = dot_nt(branch, wo_ref[...]).astype(jnp.bfloat16)


def feed(inputs, attn_out, grads, gain, w_out, w_in, turned_down, block):
    rows, width = inputs.shape
    by_rows = lambda columns: pl.BlockSpec((block, columns), lambda i: (i, 0))
    whole = lambda array: pl.BlockSpec(array.shape, lambda i: (0, 0))
    like = lambda columns, kind=jnp.bfloat16: jax.ShapeDtypeStruct((rows, columns), kind)
    return pl.pallas_call(
        feed_kernel,
        grid=(rows // block,),
        in_specs=[by_rows(width)] * 3 + [whole(item) for item in (gain, w_out, w_in, turned_down)],
        out_specs=[
            by_rows(width),
            by_rows(width),
            by_rows(FF),
            by_rows(2 * FF),
            by_rows(width),
            by_rows(width),
            by_rows(width),
            pl.BlockSpec((8, width), lambda i: (0, 0)),
        ],
        out_shape=[
            like(width),
            like(width),
            like(FF),
            like(2 * FF),
            like(width, jnp.float32),
            like(width),
            like(width),
            jax.ShapeDtypeStruct((8, width), jnp.float32),
        ],
        compiler_params=pltpu.CompilerParams(vmem_limit_bytes=VMEM_LIMIT),
        cost_estimate=pl.CostEstimate(
            flops=4 * rows * width * (width + 3 * FF),
            bytes_accessed=30 * rows * width,
            transcendentals=2 * rows * FF,
        ),
        name="feed",
    )(inputs, attn_out, grads, gain, w_out, w_in, turned_down)


def finish_kernel(
    x_ref, ghid_ref, dq_ref, dk_ref, dv_ref, kv_ref, cos_ref, sin_ref, gain_ref, w_ref,
    raw_ref, gin_ref, ggain_ref,
):
    @pl.when(pl.program_id(0) == 0)
    def _():
        ggain_ref[...] = jnp.zeros_like(ggain_ref)

    width = x_ref.shape[1]
    cosine, sine = cos_ref[...], sin_ref[...]
    for part in range(3):
        for at in range(0, width, 2 * HD):
            if part == 0:
                chunk = dq_ref[:, at : at + 2 * HD].astype(jnp.float32)
            else:
                held = dk_ref if part == 1 else dv_ref
                start = (part - 1) * width + at
                chunk = held[:, at : at + 2 * HD].astype(jnp.float32)
                chunk = chunk + kv_ref[:, start : start + 2 * HD].astype(jnp.float32)
            if part < 2:
                chunk = chunk * cosine - half_turn(chunk) * sine
            start = part * width + at
            raw_ref[:, start : start + 2 * HD] = chunk.astype(jnp.bfloat16)
    grad_normed = dot_nt(raw_ref[...], w_ref[...])
    normed, inverse = normalize(x_ref[...].astype(jnp.float32))
    ggain_ref[0:1, :] += jnp.sum(grad_normed * normed, axis=0, keepdims=True)
    gin_ref[...] = ghid_ref[...] + norm_back(grad_normed, normed, inverse, gain_ref[...])


def finish(inputs, grad_hidden, grad_query, grad_keys, grad_values, received, cosine, sine, gain, weights, block):
    rows, width = inputs.shape
    by_rows = lambda columns: pl.BlockSpec((block, columns), lambda i: (i, 0))
    whole = lambda array: pl.BlockSpec(array.shape, lambda i: (0, 0))
    return pl.pallas_call(
        finish_kernel,
        grid=(rows // block,),
        in_specs=[by_rows(width)] * 5
        + [by_rows(2 * width), by_rows(2 * HD), by_rows(2 * HD), whole(gain), whole(weights)],
        out_specs=[
            by_rows(3 * width),
            by_rows(width),
            pl.BlockSpec((8, width), lambda i: (0, 0)),
        ],
        out_shape=[
            jax.ShapeDtypeStruct((rows, 3 * width), jnp.bfloat16),
            jax.ShapeDtypeStruct((rows, width), jnp.float32),
            jax.ShapeDtypeStruct((8, width), jnp.float32),
        ],
        compiler_params=pltpu.CompilerParams(vmem_limit_bytes=VMEM_LIMIT),
        cost_estimate=pl.CostEstimate(
            flops=6 * rows * width * width, bytes_accessed=26 * rows * width, transcendentals=0
        ),
        name="finish",
    )(inputs, grad_hidden, grad_query, grad_keys, grad_values, received, cosine, sine, gain, weights)


def swap_chips(values):
    return lax.ppermute(values, "seq", [(0, 2), (2, 0), (1, 3), (3, 1)])


def swap_cores(values):
    return lax.ppermute(values, "seq", [(0, 1), (1, 0), (2, 3), (3, 2)])


def take(values, which):
    return jnp.where(which == 0, values[0], values[1])


def gather(values):
    return lax.all_gather(values, "dp", axis=0, tiled=True)


def sum_shares(partial):
    core = lax.axis_index("seq") % 2
    half = partial.shape[1] // 2
    halves = (partial[:, :half].astype(jnp.bfloat16), partial[:, half:].astype(jnp.bfloat16))
    theirs = take(halves, 1 - core)
    mine = jnp.where(core == 0, partial[:, :half], partial[:, half:])
    mine = (mine + swap_cores(theirs).astype(jnp.float32)).astype(jnp.bfloat16)
    share = lax.psum_scatter(mine, "dp", scatter_dimension=0, tiled=True)
    share = share.astype(jnp.float32) + swap_chips(share).astype(jnp.float32)
    share = share.astype(jnp.bfloat16)
    other = swap_cores(share)
    both = jnp.where(
        core == 0,
        jnp.concatenate([share, other], axis=1),
        jnp.concatenate([other, share], axis=1),
    )
    return both.astype(jnp.float32)


def give_back(values, chip, tokens):
    mine, theirs = values[:tokens], swap_chips(values[tokens:])
    return jnp.where(chip == 0, jnp.stack([mine, theirs]), jnp.stack([theirs, mine]))


def shards(layer_input, cotangent, norm_gain1, w_qkv, w_out, norm_gain2, w_in, w_down):
    seq_count, tokens_dev, width = layer_input.shape
    index = lax.axis_index("seq")
    chip = index // 2
    rows = seq_count * tokens_dev
    sent_inputs = swap_chips(take(layer_input, 1 - chip))
    proj_qkv = gather(w_qkv)
    gains = gather(jnp.stack([norm_gain1, norm_gain2], axis=1)).astype(jnp.float32)
    gain_one, gain_two = gains[:, 0][None], gains[:, 1][None]
    proj_out = gather(w_out)
    proj_in = gather(w_in)
    turned_down = gather(w_down.T)
    inputs = jnp.concatenate([take(layer_input, chip), sent_inputs], axis=0)
    grad_output = jnp.concatenate(
        [take(cotangent, chip), swap_chips(take(cotangent, 1 - chip))], axis=0
    )
    local = jnp.arange(tokens_dev, dtype=jnp.int32)
    positions = jnp.concatenate([index * tokens_dev + local, (index ^ 2) * tokens_dev + local])
    cosine, sine = rope_tables(positions)
    half = HD // 2
    sine = jnp.concatenate([-sine[:, :half], sine[:, half:]], axis=1)
    cosine = jnp.concatenate([cosine, cosine], axis=1)
    sine = jnp.concatenate([sine, sine], axis=1)
    block = min(256, rows)
    attn_in, query, keys = project(inputs, gain_one, proj_qkv, cosine, sine, block)
    all_keys = jnp.concatenate([keys, swap_cores(keys)], axis=0)
    attn_out, lse = attend(query, all_keys, all_keys, block)
    output, ffn_in, product, grad_mixed_ffn, grad_hidden, grad_branch, grad_attn, gain_sum_two = feed(
        inputs, attn_out, grad_output, gain_two, proj_out, proj_in, turned_down, block
    )
    result = give_back(output, chip, tokens_dev)
    grad_down = contract_rows(grad_output, product)
    grad_in = contract_rows(ffn_in, grad_mixed_ffn)
    grad_proj_out = contract_rows(attn_out, grad_branch)
    early = sum_shares(jnp.concatenate([grad_in, grad_down, grad_proj_out], axis=1))
    total_in = early[:, : 2 * FF]
    total_down = early[:, 2 * FF : 3 * FF].T
    total_out = early[:, 3 * FF :]
    grad_query, grad_keys, grad_values = attend_back(
        query, grad_attn, attn_out, lse, all_keys, 512
    )
    received = swap_cores(jnp.concatenate([grad_keys[rows:], grad_values[rows:]], axis=1))
    grad_raw, grad_inputs, gain_sum_one = finish(
        inputs, grad_hidden, grad_query, grad_keys, grad_values, received,
        cosine, sine, gain_one, proj_qkv, block,
    )
    total_qkv = sum_shares(contract_rows(attn_in, grad_raw))
    grad_inputs = give_back_wide(grad_inputs, chip, tokens_dev)
    gain_totals = lax.psum(
        lax.psum_scatter(
            jnp.stack([gain_sum_one[0], gain_sum_two[0]], axis=1), "dp", scatter_dimension=0, tiled=True
        ),
        "seq",
    )
    return (
        result,
        grad_inputs,
        gain_totals[:, 0],
        total_qkv,
        total_out,
        gain_totals[:, 1],
        total_in,
        total_down,
    )


def give_back_wide(values, chip, tokens):
    mine = values[:tokens]
    theirs = swap_chips(values[tokens:].astype(jnp.bfloat16)).astype(jnp.float32)
    return jnp.where(chip == 0, jnp.stack([mine, theirs]), jnp.stack([theirs, mine]))


def solution(mesh):
    in_specs = (
        P("dp", "seq", None),
        P("dp", "seq", None),
        P("dp"),
        P("dp", None),
        P("dp", None),
        P("dp"),
        P("dp", None),
        P(None, "dp"),
    )
    out_specs = (
        P("dp", "seq", None),
        P("dp", "seq", None),
        P("dp"),
        P("dp", None),
        P("dp", None),
        P("dp"),
        P("dp", None),
        P(None, "dp"),
    )
    return jax.shard_map(shards, mesh=mesh, in_specs=in_specs, out_specs=out_specs, check_vma=False)
```

time: 998 us -> 623 us (0.62); the launches traced: 986 us -> 622 us
  matrix products: 289 us -> 20.4 us
  Pallas kernels: 0 us -> 174 us
  local copies, waits for them, and re-layouts: 191 us -> 30.7 us
  blocking collectives: 125 us -> 24.4 us
  other arithmetic: 106 us -> 36.3 us
  waiting for transfers between devices: 242 us -> 307 us
    dot_general x64 -> x0, matrix products: 264 us -> none  [the longest x8 45.4 us: one_block(): jnp.einsum('hqk,khd->qhd', grad_scores, keys, preferred_element_type=jnp....]
    pallas_call x0 -> x5, Pallas kernels: none -> 174 us  [the longest x1 71 us: attend_back(): pl.pallas_call(attend_back_kernel, grid=(pairs, length // block), in_spec...]
    all_to_all x3 -> x0, waiting for transfers between devices: 85.1 us -> none  [the longest x1 51.5 us: shards(): lax.all_to_all(sending, 'seq', split_axis=3, concat_axis=1, tiled=True)]
    all_to_all x1 -> x0, blocking collectives: 77.3 us -> none  [shards(): lax.all_to_all(grad_stack, 'seq', split_axis=1, concat_axis=3, tiled=True)]
    all_gather x4, waiting for transfers between devices: 39.2 us -> 108 us  [gather(): return lax.all_gather(values, 'dp', axis=0, tiled=True)]
    reduce_scatter x4 -> x2, waiting for transfers between devices: 79.4 us -> 139 us  [sum_shares(): share = lax.psum_scatter(mine, 'dp', scatter_dimension=0, tiled=True)]
    convert_element_type x22 -> x7, other arithmetic: 57 us -> 16.2 us  [the longest x2 12.7 us: sum_shares(): mine = (mine + swap_cores(theirs).astype(jnp.float32)).astype(jnp.bfloat16)]
    ppermute x0 -> x12, waiting for transfers between devices: none -> 40.2 us  [the longest x6 40.1 us: swap_chips(): return lax.ppermute(values, 'seq', [(0, 2), (2, 0), (1, 3), (3, 1)])]
  transfers between devices with their start and end apart: 12 -> 19, of which waited for: 6 -> 9; matrix products, arithmetic and copies ran while one was open for 53% -> 10% of each run, Pallas kernels for 0% -> 10%
where the time goes in v1:
time: 623 us; the launch traced here: 622 us
  waiting for transfers between devices  307 us (49%)
  Pallas kernels  174 us (28%)
  other arithmetic  36.3 us (6%)
  local copies, waits for them, and re-layouts  30.7 us (5%)
  blocking collectives  24.4 us (4%)
  matrix products  20.4 us (3%)
  starting transfers between devices  14.6 us (2%)
  between operations  14.4 us (2%)
    reduce_scatter x2, waiting for transfers between devices, sum_shares(): share = lax.psum_scatter(mine, 'dp', scatter_dimension=0, tiled=True)  139 us
    all_gather x4, waiting for transfers between devices, gather(): return lax.all_gather(values, 'dp', axis=0, tiled=True)  108 us
    pallas_call x1, Pallas kernels, attend_back(): pl.pallas_call(attend_back_kernel, grid=(pairs, length // block), in_spec...  71 us
    pallas_call x1, Pallas kernels, attend(): pl.pallas_call(attend_kernel, grid=(pairs, rows // block), in_specs=[pl.B...  52.3 us
    ppermute x6, waiting for transfers between devices, swap_chips(): return lax.ppermute(values, 'seq', [(0, 2), (2, 0), (1, 3), (3, 1)])  40.1 us
    pallas_call x1, Pallas kernels, feed(): pl.pallas_call(feed_kernel, grid=(rows // block,), in_specs=[by_rows(widt...  26.6 us
    dot_general x4, matrix products, contract_rows(): lax.dot_general(left, right, (((0,), (0,)), ((), ())), preferred_element_...  20.4 us
    unnamed x8, waiting for transfers between devices  20.1 us
  transfers between devices with their start and end apart: 19, of which 9 were waited for; matrix products, arithmetic and copies ran while one was open for 10% of the time, Pallas kernels for 10%

profile of v1, /device:TPU:1, one launch (start us, length us, event | category | flops | bytes accessed | tf_op | source)
XLA Modules:
  0.0 622.1 jit_solution(3534942501313630016)
XLA Ops:
  13.2 17.0 %all-gather = bf16[8,96,2]{1,2,0:T(2,128)(2,1)S(1)} all-gather(bf16[1,96,2]{1,2,0:T(2,128)(2,1)S(1)} %maximum_bitcast_fusion), channel_id=1, replica_groups=mesh['dp'=8,'seq'=4] {'dp'}, dimensions={0}, use_global_device_ids=true | all-gather | bytes 3456 | tf_op jit(solution)/shard_map/all_gather | solution.py:422
  37.0 39.5 %all-gather.6.cloned.1.call-done.w_ref = bf16[768,2304]{1,0:T(8,128)(2,1)} async-done(((bf16[96,2304]{1,0:T(8,128)(2,1)}), bf16[768,2304]{1,0:T(8,128)(2,1)}) %all-gather.6.cloned.1.call-update) | async-done | bytes 3538960 | tf_op jit(solution)/shard_map/all_gather | solution.py:422
  76.6 8.9 %project.1 = (bf16[1024,768]{1,0:T(8,128)(2,1)}, bf16[1024,768]{1,0:T(8,128)(2,1)}, bf16[1024,1536]{1,0:T(8,128)(2,1)}) custom-call(bf16[1024,768]{1,0:T(8,128)(2,1)} %pad_maximum_fusion.3.x_ref, f32[1,768]{1,0:T(1,128)} %get-tuple-element.57.gain_ref, bf16[768,2304]{1,0:T(8,128)(2,1)} %all-gather.6.cloned.1.call-done.w_ref, ...), custom_call_target="tpu_custom_call" | custom-call | flops 3623878656 | bytes 11010048 | tf_op jit(solution)/shard_map/project/pallas_call | solution.py:256
  88.5 18.1 %collective-permute-done.2 = bf16[512,768]{1,0:T(8,128)(2,1)S(1)} collective-permute-done((bf16[512,768]{1,0:T(8,128)(2,1)S(1)}, bf16[512,768]{1,0:T(8,128)(2,1)S(1)}, u32[]{:S(2)}, u32[]{:S(2)}) %collective-permute-start.2) | collective-permute-done | bytes 786464 | tf_op jit(solution)/shard_map/ppermute | solution.py:410
  108.3 2.7 copy-done.8
  111.0 52.3 %attend.1 = (bf16[1024,768]{1,0:T(8,128)(2,1)}, f32[6,8,1024]{2,1,0:T(8,128)}) custom-call(bf16[1024,768]{1,0:T(8,128)(2,1)} %get-tuple-element.27.q_ref, bf16[2048,1536]{1,0:T(8,128)(2,1)} %copy-done.8, bf16[2048,1536]{1,0:T(8,128)(2,1)} %copy-done.8), custom_call_target="tpu_custom_call" | custom-call | flops 25769803776 | bytes 9437184 | tf_op jit(solution)/shard_map/attend/pallas_call | solution.py:123
  165.3 66.3 %all-gather.10.cloned.1.call-done.wi_ref = bf16[768,2304]{1,0:T(8,128)(2,1)} async-done(((bf16[96,2304]{1,0:T(8,128)(2,1)}), bf16[768,2304]{1,0:T(8,128)(2,1)}) %all-gather.10.cloned.1.call-update) | async-done | bytes 3538960 | tf_op jit(solution)/shard_map/all_gather | solution.py:422
  231.6 26.6 %feed.1 = (bf16[1024,768]{1,0:T(8,128)(2,1)}, bf16[1024,768]{1,0:T(8,128)(2,1)}, bf16[1024,1152]{1,0:T(8,128)(2,1)}, bf16[1024,2304]{1,0:T(8,128)(2,1)}, f32[102...) custom-call(bf16[1024,768]{1,0:T(8,128)(2,1)} %pad_maximum_fusion.3.x_ref, ...), custom_call_target="tpu_custom_call" | custom-call | flops 13287555072 | bytes 23592960 | tf_op jit(solution)/shard_map/feed/pallas_call | solution.py:319
  258.1 71.0 %attend_back.1 = (bf16[1024,768]{1,0:T(8,128)(2,1)}, bf16[2048,768]{1,0:T(8,128)(2,1)}, bf16[2048,768]{1,0:T(8,128)(2,1)}) custom-call(bf16[1024,768]{1,0:T(8,128)(2,1)} %get-tuple-element.27.q_ref, bf16[1024,768]{1,0:T(8,128)(2,1)} %get-tuple-element.32.do_ref, bf16[1024,768]{1,0:T(8,128)(2,1)} %get-tuple-element.29.attn_ref.o_ref, ...), custom_call_target="tpu_custom_call" | custom-call | flops 64424509440 | bytes 18874368 | tf_op jit(solution)/shard_map/attend_back/pallas_call | solution.py:188
  335.2 5.9 fusion.6
  341.1 6.2 %fusion.8 = f32[768,2304]{1,0:T(8,128)S(1)} fusion(bf16[1024,768]{1,0:T(8,128)(2,1)S(1)} %copy-done.13, bf16[1024,2304]{1,0:T(8,128)(2,1)} %get-tuple-element.43), kind=kOutput, calls=%fused_computation.53 | convolution fusion | flops 3623878656 | bytes 13369344 | tf_op jit(solution)/shard_map/dot_general | solution.py:59
  347.4 15.6 %finish.1 = (bf16[1024,2304]{1,0:T(8,128)(2,1)}, f32[1024,768]{1,0:T(8,128)}, f32[8,768]{1,0:T(8,128)}) custom-call(bf16[1024,768]{1,0:T(8,128)(2,1)} %pad_maximum_fusion.3.x_ref, f32[1024,768]{1,0:T(8,128)} %get-tuple-element.31.ghid_ref, bf16[1024,768]{1,0:T(8,128)(2,1)} %get-tuple-element.34.dq_ref, bf16[2048,768]{1,0:T(8,128)(2,1)} %get-tuple-element.35.dk_ref, ...), custom_call_target="tpu_custom_call" | custom-call | flops 3623878656 | bytes 20447232 | tf_op jit(solution)/shard_map/finish/pallas_call | solution.py:386
  363.0 6.8 %fusion.7 = f32[768,2304]{1,0:T(8,128)S(1)} fusion(bf16[1024,768]{1,0:T(8,128)(2,1)} %get-tuple-element.40, bf16[1024,2304]{1,0:T(8,128)(2,1)} %get-tuple-element.41), kind=kOutput, calls=%fused_computation.52 | convolution fusion | flops 3623878656 | bytes 13369344 | tf_op jit(solution)/shard_map/dot_general | solution.py:59
  376.8 3.1 fusion
  379.9 5.4 copy.25
  387.8 5.2 add_convert_fusion.1
  393.1 5.6 copy.26
  398.7 7.4 %add_convert_fusion = bf16[768,2112]{1,0:T(8,128)(2,1)} fusion(bf16[768,2112]{1,0:T(8,128)(2,1)} %copy.26, f32[768,2304]{1,0:T(8,128)} %copy-done, pred[]{:T(512)S(6)} %eq.13, f32[768,768]{1,0:T(8,128)} %copy-done.4, f32[768,1152]{1,0:T(8,128)S(1)} %copy-done.2), kind=kLoop, calls=%fused_computation.2 | loop fusion | flops 9732096 | bytes 26247168 | tf_op jit(solution)/shard_map/convert_element_type | solution.py:431
  411.0 15.4 %collective-permute-done.3 = bf16[512,768]{1,0:T(8,128)(2,1)S(1)} collective-permute-done((bf16[512,768]{1,0:T(8,128)(2,1)S(1)}, bf16[512,768]{1,0:T(8,128)(2,1)S(1)}, u32[]{:S(2)}, u32[]{:S(2)}) %collective-permute-start.3) | collective-permute-done | bytes 786464 | tf_op jit(solution)/shard_map/ppermute | solution.py:410
  427.9 18.0 %reduce-scatter.10.cloned.1.call-done = f32[96,2]{1,0:T(8,128)} async-done(((f32[768,2]{1,0:T(8,128)}), f32[96,2]{1,0:T(8,128)}) %reduce-scatter.10.cloned.1.call-update) | async-done | bytes 784
  446.8 7.4 %psum.7 = f32[96,2]{0,1:T(2,128)S(1)} all-reduce(f32[96,2]{0,1:T(2,128)S(1)} %copy.29), channel_id=1, replica_groups=mesh['dp'=8,'seq'=4] {'seq'}, use_global_device_ids=true, to_apply=%region_1.2 | all-reduce | flops 192 | bytes 1536 | tf_op jit(solution)/shard_map/psum | solution.py:497
  454.7 60.3 %reduce-scatter.6.cloned.1.call-done = bf16[96,1152]{1,0:T(8,128)(2,1)} async-done(((bf16[768,1152]{1,0:T(8,128)(2,1)}), bf16[96,1152]{1,0:T(8,128)(2,1)}) %reduce-scatter.6.cloned.1.call-update) | async-done | bytes 221200 | tf_op jit(solution)/shard_map/reduce_scatter | solution.py:432
  517.5 78.6 %reduce-scatter.8.cloned.1.call-done = bf16[96,2112]{1,0:T(8,128)(2,1)} async-done(((bf16[768,2112]{1,0:T(8,128)(2,1)}), bf16[96,2112]{1,0:T(8,128)(2,1)}) %reduce-scatter.8.cloned.1.call-update) | async-done | bytes 405520 | tf_op jit(solution)/shard_map/reduce_scatter | solution.py:432
  599.7 6.6 %collective-permute-done.10 = bf16[96,2112]{1,0:T(8,128)(2,1)S(1)} collective-permute-done((bf16[96,2112]{1,0:T(8,128)(2,1)}, bf16[96,2112]{1,0:T(8,128)(2,1)S(1)}, u32[]{:S(2)}, u32[]{:S(2)}) %collective-permute-start.10) | collective-permute-done | bytes 405536 | tf_op jit(solution)/shard_map/ppermute | solution.py:410
  (110 shorter events, 57.7 us)
Async XLA Ops:
  7.2 6.0 copy-start.11
  7.2 69.4 %all-gather.6.cloned.1.call-start = ((), (), s32[]{:S(2)}) async-start(), calls=%async_computation.3 | async-start | bytes 3981312 | tf_op jit(solution)/shard_map/all_gather | solution.py:422
  7.9 155.4 %all-gather.8.cloned.1.call-start = ((), (), s32[]{:S(2)}) async-start(), calls=%async_computation.4 | async-start | bytes 1327104 | tf_op jit(solution)/shard_map/all_gather | solution.py:422
  8.7 156.6 %all-gather.12.cloned.1.call-start = ((), (), s32[]{:S(2)}) async-start(), calls=%async_computation.6 | async-start | bytes 1990656 | tf_op jit(solution)/shard_map/all_gather | solution.py:422
  9.4 222.2 %all-gather.10.cloned.1.call-start = ((), (), s32[]{:S(2)}) async-start(), calls=%async_computation.5 | async-start | bytes 3981312 | tf_op jit(solution)/shard_map/all_gather | solution.py:422
  11.0 24.8 %collective-permute-start = (bf16[512,768]{1,0:T(8,128)(2,1)S(1)}, bf16[512,768]{1,0:T(8,128)(2,1)S(1)}, u32[]{:S(2)}, u32[]{:S(2)}) collective-permute-start(bf16[512,768]{1,0:T(8,128)(2,1)S(1)} %get-tuple-element.51), channel_id=1, source_target_pairs={{0,2},{2,0},{1,3},{3,1},{4,6},{6,4},{5,7},{7,5},{8,10},{10,8},{9,1... | collective-permute-start | bytes 2359304 | tf_op jit(solution)/shard_map/ppermute | solution.py:410
  13.1 432.8 %reduce-scatter.10.cloned.1.call-start = ((), (), s32[]{:S(2)}) async-start(), calls=%async_computation.9 | async-start | bytes 442368
  76.5 10.6 %copy-start.9 = (bf16[2,512,768]{2,1,0:T(8,128)(2,1)S(1)}, bf16[2,512,768]{2,1,0:T(8,128)(2,1)}, u32[]{:S(2)}) copy-start(bf16[2,512,768]{2,1,0:T(8,128)(2,1)} %param.9) | copy-start | bytes 4718596
  85.5 22.4 %copy-start.6 = (bf16[1024,1536]{1,0:T(8,128)(2,1)S(1)}, bf16[1024,1536]{1,0:T(8,128)(2,1)}, u32[]{:S(2)}) copy-start(bf16[1024,1536]{1,0:T(8,128)(2,1)} %get-tuple-element.28) | copy-start | bytes 9437188
  85.5 22.6 %collective-permute-start.1 = (bf16[1024,1536]{1,0:T(8,128)(2,1)}, bf16[1024,1536]{1,0:T(8,128)(2,1)S(1)}, u32[]{:S(2)}, u32[]{:S(2)}) collective-permute-start(bf16[1024,1536]{1,0:T(8,128)(2,1)} %get-tuple-element.28), channel_id=1, source_target_pairs={{0,1},{1,0},{2,3},{3,2},{4,5},{5,4},{6,7},{7,6},{8,9},{9,8},{10,11... | collective-permute-start | bytes 9437192 | tf_op jit(solution)/shard_map/ppermute | solution.py:414
  87.2 19.3 %collective-permute-start.2 = (bf16[512,768]{1,0:T(8,128)(2,1)S(1)}, bf16[512,768]{1,0:T(8,128)(2,1)S(1)}, u32[]{:S(2)}, u32[]{:S(2)}) collective-permute-start(bf16[512,768]{1,0:T(8,128)(2,1)S(1)} %get-tuple-element.49), channel_id=1, source_target_pairs={{0,2},{2,0},{1,3},{3,1},{4,6},{6,4},{5,7},{7,5},{8,10},{10,8},{9,1... | collective-permute-start | bytes 2359304 | tf_op jit(solution)/shard_map/ppermute | solution.py:410
  333.6 13.8 %collective-permute-start.4 = (bf16[1024,1536]{1,0:T(8,128)(2,1)}, bf16[1024,1536]{1,0:T(8,128)(2,1)}, u32[]{:S(2)}, u32[]{:S(2)}) collective-permute-start(bf16[1024,1536]{1,0:T(8,128)(2,1)} %pad_maximum_fusion.2), channel_id=1, source_target_pairs={{0,1},{1,0},{2,3},{3,2},{4,5},{5,4},{6,7},{7,6},{8,9},{9,8},{10,11... | collective-permute-start | bytes 9437192 | tf_op jit(solution)/shard_map/ppermute | solution.py:414
  347.4 28.0 %copy-start = (f32[768,2304]{1,0:T(8,128)}, f32[768,2304]{1,0:T(8,128)S(1)}, u32[]{:S(2)}) copy-start(f32[768,2304]{1,0:T(8,128)S(1)} %fusion.8) | copy-start | bytes 21233668
  371.3 16.5 %collective-permute-start.6 = (bf16[768,1152]{1,0:T(8,128)(2,1)}, bf16[768,1152]{1,0:T(8,128)(2,1)}, u32[]{:S(2)}, u32[]{:S(2)}) collective-permute-start(bf16[768,1152]{1,0:T(8,128)(2,1)} %fusion.1), channel_id=1, source_target_pairs={{0,1},{1,0},{2,3},{3,2},{4,5},{5,4},{6,7},{7,6},{8,9},{9,8},{10,11... | collective-permute-start | bytes 5308424 | tf_op jit(solution)/shard_map/ppermute | solution.py:414
  385.3 7.9 %collective-permute-start.9 = (bf16[768,2112]{0,1:T(8,128)(2,1)}, bf16[768,2112]{0,1:T(8,128)(2,1)}, u32[]{:S(2)}, u32[]{:S(2)}) collective-permute-start(bf16[768,2112]{0,1:T(8,128)(2,1)} %copy.25), channel_id=1, source_target_pairs={{0,1},{1,0},{2,3},{3,2},{4,5},{5,4},{6,7},{7,6},{8,9},{9,8},{10,11... | collective-permute-start | bytes 9732104 | tf_op jit(solution)/shard_map/ppermute | solution.py:414
  387.7 127.3 %reduce-scatter.6.cloned.1.call-start = ((), (), s32[]{:S(2)}) async-start(), calls=%async_computation.7 | async-start | bytes 1990656 | tf_op jit(solution)/shard_map/reduce_scatter | solution.py:432
  393.1 203.0 %reduce-scatter.8.cloned.1.call-start = ((), (), s32[]{:S(2)}) async-start(), calls=%async_computation.8 | async-start | bytes 3760128 | tf_op jit(solution)/shard_map/reduce_scatter | solution.py:432
  407.7 20.1 %copy-start.7 = (f32[1024,768]{1,0:T(8,128)S(1)}, f32[1024,768]{1,0:T(8,128)}, u32[]{:S(2)}) copy-start(f32[1024,768]{1,0:T(8,128)} %get-tuple-element.37) | copy-start | bytes 9437188
  407.7 18.7 %collective-permute-start.3 = (bf16[512,768]{1,0:T(8,128)(2,1)S(1)}, bf16[512,768]{1,0:T(8,128)(2,1)S(1)}, u32[]{:S(2)}, u32[]{:S(2)}) collective-permute-start(bf16[512,768]{1,0:T(8,128)(2,1)S(1)} %get-tuple-element.47), channel_id=1, source_target_pairs={{0,2},{2,0},{1,3},{3,1},{4,6},{6,4},{5,7},{7,5},{8,10},{10,8},{9,1... | collective-permute-start | bytes 2359304 | tf_op jit(solution)/shard_map/ppermute | solution.py:410
  410.5 105.8 %collective-permute-start.5 = (bf16[512,768]{1,0:T(8,128)(2,1)S(1)}, bf16[512,768]{1,0:T(8,128)(2,1)}, u32[]{:S(2)}, u32[]{:S(2)}) collective-permute-start(bf16[512,768]{1,0:T(8,128)(2,1)S(1)} %slice.151), channel_id=1, source_target_pairs={{0,2},{2,0},{1,3},{3,1},{4,6},{6,4},{5,7},{7,5},{8,10},{10,8},{9,1... | collective-permute-start | bytes 2359304 | tf_op jit(solution)/shard_map/ppermute | solution.py:410
  515.0 82.3 %collective-permute-start.7 = (bf16[96,1152]{1,0:T(8,128)(2,1)}, bf16[96,1152]{1,0:T(8,128)(2,1)S(1)}, u32[]{:S(2)}, u32[]{:S(2)}) collective-permute-start(bf16[96,1152]{1,0:T(8,128)(2,1)} %reduce-scatter.6.cloned.1.call-done), channel_id=1, source_target_pairs={{0,2},{2,0},{1,3},{3,1},{4,6},{6,4},{5,7},{7,5},{8,10},{10,8},{9,1... | collective-permute-start | bytes 663560 | tf_op jit(solution)/shard_map/ppermute | solution.py:410
  596.1 10.3 %collective-permute-start.10 = (bf16[96,2112]{1,0:T(8,128)(2,1)}, bf16[96,2112]{1,0:T(8,128)(2,1)S(1)}, u32[]{:S(2)}, u32[]{:S(2)}) collective-permute-start(bf16[96,2112]{1,0:T(8,128)(2,1)} %reduce-scatter.8.cloned.1.call-done), channel_id=1, source_target_pairs={{0,2},{2,0},{1,3},{3,1},{4,6},{6,4},{5,7},{7,5},{8,10},{10,8},{9,1... | collective-permute-start | bytes 1216520 | tf_op jit(solution)/shard_map/ppermute | solution.py:410
  598.3 13.1 %collective-permute-start.8 = (bf16[96,1152]{1,0:T(8,128)(2,1)S(1)}, bf16[96,1152]{1,0:T(8,128)(2,1)S(1)}, u32[]{:S(2)}, u32[]{:S(2)}) collective-permute-start(bf16[96,1152]{1,0:T(8,128)(2,1)S(1)} %add_convert_fusion.3), channel_id=1, source_target_pairs={{0,1},{1,0},{2,3},{3,2},{4,5},{5,4},{6,7},{7,6},{8,9},{9,8},{10,11... | collective-permute-start | bytes 663560 | tf_op jit(solution)/shard_map/ppermute | solution.py:414
  607.4 5.0 collective-permute-start.11
  (11 other events, 40.6 us)
Sparse Core Ops, SparseCore 0:
  10.2 66.2 all-gather.5
  78.7 39.3 all-gather.7
  120.3 44.9 all-gather.11
  167.3 64.2 all-gather.9
  387.9 57.9 reduce-scatter.9
  449.2 65.7 reduce-scatter.5
  519.1 76.9 reduce-scatter.7

commit v2 on v1

--- a/solution.py
+++ b/solution.py
@@ -116,15 +116,16 @@
     lse_ref[0, 1:2, :] = turned[HD : HD + 1]
 
 
-def attend(query, keys, values, block):
-    rows, width = query.shape
+def attend(query, keys, block, first):
+    rows = query.shape[0]
     length = keys.shape[0]
+    width = keys.shape[1] // 2
     pairs = width // (2 * HD)
     return pl.pallas_call(
         attend_kernel,
         grid=(pairs, rows // block),
         in_specs=[
-            pl.BlockSpec((block, 2 * HD), lambda p, i: (i, p)),
+            pl.BlockSpec((block, 2 * HD), lambda p, i: (i, p + first)),
             pl.BlockSpec((length, 2 * HD), lambda p, i: (0, p)),
             pl.BlockSpec((length, 2 * HD), lambda p, i: (0, p + pairs)),
         ],
@@ -144,7 +145,7 @@
             transcendentals=rows * length * width // HD,
         ),
         name="attend",
-    )(query, keys, values)
+    )(query, keys, keys)
 
 
 def attend_back_kernel(
@@ -180,24 +181,25 @@
         dq_ref[...] = (acc_ref[...].T * SCALE).astype(jnp.bfloat16)
 
 
-def attend_back(query, grads, outs, lse, keys, block):
-    rows, width = query.shape
+def attend_back(query, grads, outs, lse, keys, block, first):
+    rows = query.shape[0]
     length = keys.shape[0]
+    width = keys.shape[1] // 2
     pairs = width // (2 * HD)
-    own = pl.BlockSpec((rows, 2 * HD), lambda p, i: (0, p))
+    own = pl.BlockSpec((rows, 2 * HD), lambda p, i: (0, p + first))
     return pl.pallas_call(
         attend_back_kernel,
         grid=(pairs, length // block),
         in_specs=[
             own,
             own,
-            own,
+            pl.BlockSpec((rows, 2 * HD), lambda p, i: (0, p)),
             pl.BlockSpec((1, 8, rows), lambda p, i: (p, 0, 0)),
             pl.BlockSpec((block, 2 * HD), lambda p, i: (i, p)),
             pl.BlockSpec((block, 2 * HD), lambda p, i: (i, p + pairs)),
         ],
         out_specs=[
-            own,
+            pl.BlockSpec((rows, 2 * HD), lambda p, i: (0, p)),
             pl.BlockSpec((block, 2 * HD), lambda p, i: (i, p)),
             pl.BlockSpec((block, 2 * HD), lambda p, i: (i, p)),
         ],
@@ -234,19 +236,24 @@
     return jnp.where(lanes % HD < half, ahead, behind)
 
 
-def project_kernel(x_ref, gain_ref, w_ref, cos_ref, sin_ref, in_ref, q_ref, kv_ref):
+def project_kernel(x_ref, gain_ref, w_ref, cos_ref, sin_ref, in_ref, q_ref, one_ref, two_ref):
     normed, _ = normalize(x_ref[...].astype(jnp.float32))
     attn_in = (normed * gain_ref[...]).astype(jnp.bfloat16)
     in_ref[...] = attn_in
     width = x_ref.shape[1]
     cosine, sine = cos_ref[...], sin_ref[...]
-    for part, target, start in ((0, q_ref, 0), (1, kv_ref, 0), (2, kv_ref, width)):
+    share = width // 2
+    for part in range(3):
         mixed = dot_nn(attn_in, w_ref[:, part * width : (part + 1) * width])
         for at in range(0, width, 2 * HD):
             chunk = mixed[:, at : at + 2 * HD]
             if part < 2:
                 chunk = chunk * cosine + half_turn(chunk) * sine
-            target[:, start + at : start + at + 2 * HD] = chunk.astype(jnp.bfloat16)
+            target, start = (q_ref, at)
+            if part > 0:
+                target = (one_ref, two_ref)[at // share]
+                start = (part - 1) * share + at % share
+            target[:, start : start + 2 * HD] = chunk.astype(jnp.bfloat16)
 
 
 def project(inputs, gain, weights, cosine, sine, block):
@@ -263,12 +270,8 @@
             by_rows(2 * HD),
             by_rows(2 * HD),
         ],
-        out_specs=[by_rows(width), by_rows(width), by_rows(2 * width)],
-        out_shape=[
-            jax.ShapeDtypeStruct((rows, width), jnp.bfloat16),
-            jax.ShapeDtypeStruct((rows, width), jnp.bfloat16),
-            jax.ShapeDtypeStruct((rows, 2 * width), jnp.bfloat16),
-        ],
+        out_specs=[by_rows(width)] * 4,
+        out_shape=[jax.ShapeDtypeStruct((rows, width), jnp.bfloat16)] * 4,
         compiler_params=pltpu.CompilerParams(vmem_limit_bytes=VMEM_LIMIT),
         cost_estimate=pl.CostEstimate(
             flops=6 * rows * width * width, bytes_accessed=14 * rows * width, transcendentals=0
@@ -278,7 +281,7 @@
 
 
 def feed_kernel(
-    x_ref, attn_ref, g_ref, gain_ref, wo_ref, wi_ref, wd_ref,
+    x_ref, one_ref, two_ref, g_ref, gain_ref, wo_ref, wi_ref, wd_ref,
     out_ref, fin_ref, prod_ref, gmix_ref, ghid_ref, gbr_ref, gattn_ref, ggain_ref,
 ):
     @pl.when(pl.program_id(0) == 0)
@@ -286,7 +289,8 @@
         ggain_ref[...] = jnp.zeros_like(ggain_ref)
 
     gain = gain_ref[...]
-    hidden = x_ref[...].astype(jnp.float32) + dot_nn(attn_ref[...], wo_ref[...])
+    attn = jnp.concatenate([one_ref[...], two_ref[...]], axis=1)
+    hidden = x_ref[...].astype(jnp.float32) + dot_nn(attn, wo_ref[...])
     normed, inverse = normalize(hidden)
     ffn_in = (normed * gain).astype(jnp.bfloat16)
     fin_ref[...] = ffn_in
@@ -311,7 +315,7 @@
     gattn_ref[...] = dot_nt(branch, wo_ref[...]).astype(jnp.bfloat16)
 
 
-def feed(inputs, attn_out, grads, gain, w_out, w_in, turned_down, block):
+def feed(inputs, attn_one, attn_two, grads, gain, w_out, w_in, turned_down, block):
     rows, width = inputs.shape
     by_rows = lambda columns: pl.BlockSpec((block, columns), lambda i: (i, 0))
     whole = lambda array: pl.BlockSpec(array.shape, lambda i: (0, 0))
@@ -319,7 +323,9 @@
     return pl.pallas_call(
         feed_kernel,
         grid=(rows // block,),
-        in_specs=[by_rows(width)] * 3 + [whole(item) for item in (gain, w_out, w_in, turned_down)],
+        in_specs=[by_rows(width), by_rows(width // 2), by_rows(width // 2), by_rows(width)]
+        + [whole(item) for item in (gain, w_out, w_in)]
+        + [pl.BlockSpec((width, FF), lambda i: (0, 0))],
         out_specs=[
             by_rows(width),
             by_rows(width),
@@ -347,27 +353,29 @@
             transcendentals=2 * rows * FF,
         ),
         name="feed",
-    )(inputs, attn_out, grads, gain, w_out, w_in, turned_down)
-
-
-def finish_kernel(
-    x_ref, ghid_ref, dq_ref, dk_ref, dv_ref, kv_ref, cos_ref, sin_ref, gain_ref, w_ref,
-    raw_ref, gin_ref, ggain_ref,
-):
+    )(inputs, attn_one, attn_two, grads, gain, w_out, w_in, turned_down)
+
+
+def finish_kernel(*refs):
+    x_ref, ghid_ref = refs[:2]
+    parts = (refs[2:6], refs[6:10])
+    cos_ref, sin_ref, gain_ref, w_ref, raw_ref, gin_ref, ggain_ref = refs[10:]
+
     @pl.when(pl.program_id(0) == 0)
     def _():
         ggain_ref[...] = jnp.zeros_like(ggain_ref)
 
     width = x_ref.shape[1]
+    share = width // 2
     cosine, sine = cos_ref[...], sin_ref[...]
     for part in range(3):
         for at in range(0, width, 2 * HD):
-            if part == 0:
-                chunk = dq_ref[:, at : at + 2 * HD].astype(jnp.float32)
-            else:
-                held = dk_ref if part == 1 else dv_ref
-                start = (part - 1) * width + at
-                chunk = held[:, at : at + 2 * HD].astype(jnp.float32)
+            dq_ref, dk_ref, dv_ref, kv_ref = parts[at // share]
+            here = at % share
+            held = (dq_ref, dk_ref, dv_ref)[part]
+            chunk = held[:, here : here + 2 * HD].astype(jnp.float32)
+            if part > 0:
+                start = (part - 1) * share + here
                 chunk = chunk + kv_ref[:, start : start + 2 * HD].astype(jnp.float32)
             if part < 2:
                 chunk = chunk * cosine - half_turn(chunk) * sine
@@ -379,15 +387,16 @@
     gin_ref[...] = ghid_ref[...] + norm_back(grad_normed, normed, inverse, gain_ref[...])
 
 
-def finish(inputs, grad_hidden, grad_query, grad_keys, grad_values, received, cosine, sine, gain, weights, block):
+def finish(inputs, grad_hidden, parts, cosine, sine, gain, weights, block):
     rows, width = inputs.shape
     by_rows = lambda columns: pl.BlockSpec((block, columns), lambda i: (i, 0))
     whole = lambda array: pl.BlockSpec(array.shape, lambda i: (0, 0))
     return pl.pallas_call(
         finish_kernel,
         grid=(rows // block,),
-        in_specs=[by_rows(width)] * 5
-        + [by_rows(2 * width), by_rows(2 * HD), by_rows(2 * HD), whole(gain), whole(weights)],
+        in_specs=[by_rows(width)] * 2
+        + ([by_rows(width // 2)] * 3 + [by_rows(width)]) * 2
+        + [by_rows(2 * HD), by_rows(2 * HD), whole(gain), whole(weights)],
         out_specs=[
             by_rows(3 * width),
             by_rows(width),
@@ -403,7 +412,7 @@
             flops=6 * rows * width * width, bytes_accessed=26 * rows * width, transcendentals=0
         ),
         name="finish",
-    )(inputs, grad_hidden, grad_query, grad_keys, grad_values, received, cosine, sine, gain, weights)
+    )(inputs, grad_hidden, *parts[0], *parts[1], cosine, sine, gain, weights)
 
 
 def swap_chips(values):
@@ -418,27 +427,35 @@
     return jnp.where(which == 0, values[0], values[1])
 
 
-def gather(values):
-    return lax.all_gather(values, "dp", axis=0, tiled=True)
-
-
-def sum_shares(partial):
+def by_core(values):
     core = lax.axis_index("seq") % 2
-    half = partial.shape[1] // 2
-    halves = (partial[:, :half].astype(jnp.bfloat16), partial[:, half:].astype(jnp.bfloat16))
-    theirs = take(halves, 1 - core)
-    mine = jnp.where(core == 0, partial[:, :half], partial[:, half:])
-    mine = (mine + swap_cores(theirs).astype(jnp.float32)).astype(jnp.bfloat16)
-    share = lax.psum_scatter(mine, "dp", scatter_dimension=0, tiled=True)
-    share = share.astype(jnp.float32) + swap_chips(share).astype(jnp.float32)
+    half = values.shape[1] // 2
+    first, second = values[:, :half], values[:, half:]
+    return jnp.where(core == 0, first, second), jnp.where(core == 0, second, first)
+
+
+def join_cores(mine, theirs):
+    core = lax.axis_index("seq") % 2
+    first = jnp.where(core == 0, mine, theirs)
+    second = jnp.where(core == 0, theirs, mine)
+    return jnp.concatenate([first, second], axis=1)
+
+
+def send_rows(values):
+    parts = lax.axis_size("dp")
+    pieces = values.reshape(parts, values.shape[0] // parts, values.shape[1])
+    return lax.all_to_all(pieces, "dp", split_axis=0, concat_axis=0, tiled=True)
+
+
+def finish_halves(pieces):
+    share = jnp.sum(pieces.astype(jnp.float32), axis=0)
+    share = share + swap_chips(share.astype(jnp.bfloat16)).astype(jnp.float32)
     share = share.astype(jnp.bfloat16)
-    other = swap_cores(share)
-    both = jnp.where(
-        core == 0,
-        jnp.concatenate([share, other], axis=1),
-        jnp.concatenate([other, share], axis=1),
-    )
-    return both.astype(jnp.float32)
+    return share, swap_cores(share)
+
+
+def finish_sum(pieces):
+    return join_cores(*finish_halves(pieces)).astype(jnp.float32)
 
 
 def give_back(values, chip, tokens):
@@ -452,12 +469,23 @@
     chip = index // 2
     rows = seq_count * tokens_dev
     sent_inputs = swap_chips(take(layer_input, 1 - chip))
-    proj_qkv = gather(w_qkv)
-    gains = gather(jnp.stack([norm_gain1, norm_gain2], axis=1)).astype(jnp.float32)
+    columns = w_qkv.shape[1] // 2
+    column = lambda values: jnp.pad(values[:, None], ((0, 0), (0, 2 * HD - 1)))
+    own_qkv, _ = by_core(
+        jnp.concatenate(
+            [w_qkv[:, :columns], column(norm_gain1), w_qkv[:, columns:], column(norm_gain2)], axis=1
+        )
+    )
+    half_qkv = lax.all_gather(own_qkv, "dp", axis=0, tiled=True)
+    other_qkv = swap_cores(half_qkv)
+    proj_qkv = join_cores(half_qkv[:, :columns], other_qkv[:, :columns])
+    gains = join_cores(half_qkv[:, columns : columns + 1], other_qkv[:, columns : columns + 1])
+    gains = gains.astype(jnp.float32)
     gain_one, gain_two = gains[:, 0][None], gains[:, 1][None]
-    proj_out = gather(w_out)
-    proj_in = gather(w_in)
-    turned_down = gather(w_down.T)
+    down = -(-FF // (4 * HD)) * 4 * HD
+    padded = lambda values: jnp.pad(values, ((0, 0), (0, down - FF)))
+    halves = [by_core(item)[0] for item in (w_in, w_out, padded(w_down.T))]
+    half_rest = lax.all_gather(jnp.concatenate(halves, axis=1), "dp", axis=0, tiled=True)
     inputs = jnp.concatenate([take(layer_input, chip), sent_inputs], axis=0)
     grad_output = jnp.concatenate(
         [take(cotangent, chip), swap_chips(take(cotangent, 1 - chip))], axis=0
@@ -470,43 +498,96 @@
     cosine = jnp.concatenate([cosine, cosine], axis=1)
     sine = jnp.concatenate([sine, sine], axis=1)
     block = min(256, rows)
-    attn_in, query, keys = project(inputs, gain_one, proj_qkv, cosine, sine, block)
-    all_keys = jnp.concatenate([keys, swap_cores(keys)], axis=0)
-    attn_out, lse = attend(query, all_keys, all_keys, block)
+    split = width // (4 * HD)
+    attn_in, query, *keys = project(inputs, gain_one, proj_qkv, cosine, sine, block)
+    keys = [jnp.concatenate([item, swap_cores(item)], axis=0) for item in keys]
+    attn_one, lse_one = attend(query, keys[0], block, 0)
+    half_rest, attn_one = lax.optimization_barrier((half_rest, attn_one))
+    other_rest = swap_cores(half_rest)
+    attn_two, lse_two = attend(query, keys[1], block, split)
+    proj_in = join_cores(half_rest[:, :FF], other_rest[:, :FF])
+    cut = FF + width // 2
+    proj_out = join_cores(half_rest[:, FF:cut], other_rest[:, FF:cut])
+    turned_down = join_cores(half_rest[:, cut:], other_rest[:, cut:])
     output, ffn_in, product, grad_mixed_ffn, grad_hidden, grad_branch, grad_attn, gain_sum_two = feed(
-        inputs, attn_out, grad_output, gain_two, proj_out, proj_in, turned_down, block
+        inputs, attn_one, attn_two, grad_output, gain_two, proj_out, proj_in, turned_down, block
     )
     result = give_back(output, chip, tokens_dev)
-    grad_down = contract_rows(grad_output, product)
-    grad_in = contract_rows(ffn_in, grad_mixed_ffn)
-    grad_proj_out = contract_rows(attn_out, grad_branch)
-    early = sum_shares(jnp.concatenate([grad_in, grad_down, grad_proj_out], axis=1))
-    total_in = early[:, : 2 * FF]
-    total_down = early[:, 2 * FF : 3 * FF].T
-    total_out = early[:, 3 * FF :]
-    grad_query, grad_keys, grad_values = attend_back(
-        query, grad_attn, attn_out, lse, all_keys, 512
-    )
-    received = swap_cores(jnp.concatenate([grad_keys[rows:], grad_values[rows:]], axis=1))
+
+    def ready(mine, theirs):
+        return (mine + theirs.astype(jnp.float32)).astype(jnp.bfloat16)
+
+    in_mine, in_theirs = by_core(contract_rows(ffn_in, grad_mixed_ffn))
+    in_theirs = in_theirs.astype(jnp.bfloat16)
+    in_theirs, product, grad_branch = lax.optimization_barrier((in_theirs, product, grad_branch))
+    in_got = swap_cores(in_theirs)
+    grad_down = padded(contract_rows(grad_output, product))
+    grad_proj_out = jnp.concatenate(
+        [contract_rows(attn_one, grad_branch), contract_rows(attn_two, grad_branch)], axis=0
+    )
+    down_mine, down_theirs = by_core(grad_down)
+    out_mine, out_theirs = by_core(grad_proj_out)
+    rest_theirs = jnp.concatenate([down_theirs, out_theirs], axis=1).astype(jnp.bfloat16)
+    in_sum = ready(in_mine, in_got)
+    in_sum, rest_theirs, grad_attn = lax.optimization_barrier((in_sum, rest_theirs, grad_attn))
+    in_pieces = send_rows(in_sum)
+    rest_got = swap_cores(rest_theirs)
+    kv_block = min(512, 2 * rows)
+
+    def back_part(grads, attn_out, lse, held, first):
+        grad_query, grad_keys, grad_values = attend_back(
+            query, grads, attn_out, lse, held, kv_block, first
+        )
+        received = swap_cores(jnp.concatenate([grad_keys[rows:], grad_values[rows:]], axis=1))
+        return (grad_query, grad_keys, grad_values, received)
+
+    part_one = back_part(grad_attn, attn_one, lse_one, keys[0], 0)
+    rest_sum = ready(jnp.concatenate([down_mine, out_mine], axis=1), rest_got)
+    rest_sum, in_pieces, grad_attn, result, _ = lax.optimization_barrier(
+        (rest_sum, in_pieces, grad_attn, result, part_one[0])
+    )
+    rest_pieces = send_rows(rest_sum)
+    part_two = back_part(grad_attn, attn_two, lse_two, keys[1], split)
+    rest_pieces, last_query = lax.optimization_barrier((rest_pieces, part_two[0]))
+    part_two = (last_query, *part_two[1:])
     grad_raw, grad_inputs, gain_sum_one = finish(
-        inputs, grad_hidden, grad_query, grad_keys, grad_values, received,
-        cosine, sine, gain_one, proj_qkv, block,
-    )
-    total_qkv = sum_shares(contract_rows(attn_in, grad_raw))
+        inputs, grad_hidden, (part_one, part_two), cosine, sine, gain_one, proj_qkv, block
+    )
+    grad_proj_qkv = contract_rows(attn_in, grad_raw)
+    late_mine, late_theirs = by_core(
+        jnp.concatenate(
+            [
+                grad_proj_qkv[:, :columns],
+                column(gain_sum_one[0]),
+                grad_proj_qkv[:, columns:],
+                column(gain_sum_two[0]),
+            ],
+            axis=1,
+        )
+    )
+    late_got = swap_cores(late_theirs.astype(jnp.bfloat16))
+    late_sum = ready(late_mine, late_got)
     grad_inputs = give_back_wide(grad_inputs, chip, tokens_dev)
-    gain_totals = lax.psum(
-        lax.psum_scatter(
-            jnp.stack([gain_sum_one[0], gain_sum_two[0]], axis=1), "dp", scatter_dimension=0, tiled=True
-        ),
-        "seq",
-    )
+    late_sum, grad_inputs = lax.optimization_barrier((late_sum, grad_inputs))
+    late_pieces = send_rows(late_sum)
+    total_in = finish_sum(in_pieces)
+    rest_mine, rest_other = finish_halves(rest_pieces)
+    half_down = down // 2
+    total_down = join_cores(rest_mine[:, :half_down], rest_other[:, :half_down])[:, :FF]
+    total_down = total_down.T.astype(jnp.float32)
+    total_out = join_cores(rest_mine[:, half_down:], rest_other[:, half_down:]).astype(jnp.float32)
+    late = finish_sum(late_pieces)
+    total_qkv = jnp.concatenate(
+        [late[:, :columns], late[:, columns + 2 * HD : 2 * columns + 2 * HD]], axis=1
+    )
+    total_one, total_two = late[:, columns], late[:, 2 * columns + 2 * HD]
     return (
         result,
         grad_inputs,
-        gain_totals[:, 0],
+        total_one,
         total_qkv,
         total_out,
-        gain_totals[:, 1],
+        total_two,
         total_in,
         total_down,
     )

time: 623 us -> 472 us (0.76)
  waiting for transfers between devices: 307 us -> 152 us
  starting transfers between devices: 14.6 us -> 49.9 us
  blocking collectives: 24.4 us -> 0 us
  local copies, waits for them, and re-layouts: 30.7 us -> 18.2 us
    reduce_scatter x2 -> x0, waiting for transfers between devices: 139 us -> none  [sum_shares(): share = lax.psum_scatter(mine, 'dp', scatter_dimension=0, tiled=True)]
    all_gather x4 -> x2, waiting for transfers between devices: 108 us -> 49.1 us  [the longest x1 49.1 us: shards(): half_qkv = lax.all_gather(own_qkv, 'dp', axis=0, tiled=True)]
    ppermute x6 -> x7, waiting for transfers between devices: 40.1 us -> 72.8 us  [swap_chips(): return lax.ppermute(values, 'seq', [(0, 2), (2, 0), (1, 3), (3, 1)])]
    all_to_all x0 -> x3, starting transfers between devices: none -> 27.4 us  [send_rows(): return lax.all_to_all(pieces, 'dp', split_axis=0, concat_axis=0, tiled=True)]
    all_to_all x0 -> x3, waiting for transfers between devices: none -> 25.2 us  [send_rows(): return lax.all_to_all(pieces, 'dp', split_axis=0, concat_axis=0, tiled=True)]
    unnamed x8 -> x2, waiting for transfers between devices: 20.1 us -> 0.03 us
    all_gather x1 -> x0, blocking collectives: 17 us -> none  [gather(): return lax.all_gather(values, 'dp', axis=0, tiled=True)]
    concatenate x1 -> x9, other arithmetic: 1.96 us -> 11.2 us  [the longest x4 6.66 us: join_cores(): return jnp.concatenate([first, second], axis=1)]
  transfers between devices with their start and end apart: 19 -> 24, of which waited for: 9 -> 12; matrix products, arithmetic and copies ran while one was open for 10% -> 8% of each run, Pallas kernels for 10% -> 29%
where the time goes in v2:
time: 472 us; the launch traced here: 469 us
  Pallas kernels  176 us (37%)
  waiting for transfers between devices  152 us (32%)
  starting transfers between devices  49.9 us (11%)
  other arithmetic  39.8 us (8%)
  local copies, waits for them, and re-layouts  18.2 us (4%)
  matrix products  17.5 us (4%)
  between operations  14.8 us (3%)
    pallas_call x2, Pallas kernels, attend_back(): pl.pallas_call(attend_back_kernel, grid=(pairs, length // block), in_spec...  73 us
    ppermute x7, waiting for transfers between devices, swap_chips(): return lax.ppermute(values, 'seq', [(0, 2), (2, 0), (1, 3), (3, 1)])  72.8 us
    pallas_call x2, Pallas kernels, attend(): pl.pallas_call(attend_kernel, grid=(pairs, rows // block), in_specs=[pl.B...  54.5 us
    all_gather x1, waiting for transfers between devices, shards(): half_qkv = lax.all_gather(own_qkv, 'dp', axis=0, tiled=True)  49.1 us
    all_to_all x3, starting transfers between devices, send_rows(): return lax.all_to_all(pieces, 'dp', split_axis=0, concat_axis=0, tiled=True)  27.4 us
    pallas_call x1, Pallas kernels, feed(): pl.pallas_call(feed_kernel, grid=(rows // block,), in_specs=[by_rows(widt...  26.8 us
    all_to_all x3, waiting for transfers between devices, send_rows(): return lax.all_to_all(pieces, 'dp', split_axis=0, concat_axis=0, tiled=True)  25.2 us
    dot_general x5, matrix products, contract_rows(): lax.dot_general(left, right, (((0,), (0,)), ((), ())), preferred_element_...  17.5 us
  transfers between devices with their start and end apart: 24, of which 12 were waited for; matrix products, arithmetic and copies ran while one was open for 8% of the time, Pallas kernels for 29%

profile of v2, /device:TPU:1, one launch (start us, length us, event | category | flops | bytes accessed | tf_op | source)
XLA Modules:
  0.0 468.7 jit_solution(17759449380375310959)
XLA Ops:
  11.0 49.1 %all-gather.5.cloned.1.call-done = bf16[768,1280]{1,0:T(8,128)(2,1)} async-done(((bf16[96,1280]{1,0:T(8,128)(2,1)}), bf16[768,1280]{1,0:T(8,128)(2,1)}) %all-gather.5.cloned.1.call-update) | async-done | bytes 1966096 | tf_op jit(solution)/shard_map/all_gather | solution.py:479
  69.2 13.3 %collective-permute-done.1 = bf16[512,768]{1,0:T(8,128)(2,1)S(1)} collective-permute-done((bf16[512,768]{1,0:T(8,128)(2,1)}, bf16[512,768]{1,0:T(8,128)(2,1)S(1)}, u32[]{:S(2)}, u32[]{:S(2)}) %collective-permute-start.1) | collective-permute-done | bytes 786464 | tf_op jit(solution)/shard_map/ppermute | solution.py:419
  89.6 8.9 %project.1 = (bf16[1024,768]{1,0:T(8,128)(2,1)}, bf16[1024,768]{1,0:T(8,128)(2,1)}, bf16[1024,768]{1,0:T(8,128)(2,1)}, bf16[1024,768]{1,0:T(8,128)(2,1)}) custom-call(bf16[1024,768]{1,0:T(8,128)(2,1)} %pad_maximum_fusion.4.x_ref.refs_0_, f32[1,768]{1,0:T(1,128)} %get-tuple-element.127.gain_ref.refs_12_, bf16[768,2304]{1,0:T(8,128)(2,1)} %pad_maximum_fusion.w_ref.refs_13_, ...), custom_call_target="tpu_custom_call" | custom-call | flops 3623878656 | bytes 11010048 | tf_op jit(solution)/shard_map/project/pallas_call | solution.py:263
  104.2 27.2 %attend.2 = (bf16[1024,384]{1,0:T(8,128)(2,1)}, f32[3,8,1024]{2,1,0:T(8,128)}) custom-call(bf16[1024,768]{1,0:T(8,128)(2,1)} %get-tuple-element.49.q_ref, bf16[2048,768]{1,0:T(8,128)(2,1)} %copy-done.15, bf16[2048,768]{1,0:T(8,128)(2,1)} %copy-done.15), custom_call_target="tpu_custom_call" | custom-call | flops 12884901888 | bytes 4718592 | tf_op jit(solution)/shard_map/attend/pallas_call | solution.py:124
  133.3 17.5 %collective-permute-done = bf16[512,768]{1,0:T(8,128)(2,1)S(1)} collective-permute-done((bf16[512,768]{1,0:T(8,128)(2,1)S(1)}, bf16[512,768]{1,0:T(8,128)(2,1)S(1)}, u32[]{:S(2)}, u32[]{:S(2)}) %collective-permute-start) | collective-permute-done | bytes 786464 | tf_op jit(solution)/shard_map/ppermute | solution.py:419
  154.7 27.3 %attend.3 = (bf16[1024,384]{1,0:T(8,128)(2,1)}, f32[3,8,1024]{2,1,0:T(8,128)}) custom-call(bf16[1024,768]{1,0:T(8,128)(2,1)} %get-tuple-element.49.q_ref, bf16[2048,768]{1,0:T(8,128)(2,1)} %constant_dynamic-update-slice_fusion.2.k_ref.v_ref, bf16[2048,768]{1,0:T(8,128)(2,1)} %constant_dynamic-update-slice_fusion.2.k_ref.v_ref), custom_call_target="tpu_custom_call" | custom-call | flops 12884901888 | bytes 4718592 | tf_op jit(solution)/shard_map/attend/pallas_call | solution.py:124
  187.2 26.8 %feed.1 = (bf16[1024,768]{1,0:T(8,128)(2,1)}, bf16[1024,768]{1,0:T(8,128)(2,1)}, bf16[1024,1152]{1,0:T(8,128)(2,1)}, bf16[1024,2304]{1,0:T(8,128)(2,1)}, f32[102...) custom-call(bf16[1024,768]{1,0:T(8,128)(2,1)} %pad_maximum_fusion.4.x_ref.refs_0_, ...), custom_call_target="tpu_custom_call" | custom-call | flops 13287555072 | bytes 23592960 | tf_op jit(solution)/shard_map/feed/pallas_call | solution.py:323
  214.0 6.8 %fusion.14 = f32[768,2304]{1,0:T(8,128)S(1)} fusion(bf16[1024,768]{1,0:T(8,128)(2,1)} %get-tuple-element.56, bf16[1024,2304]{1,0:T(8,128)(2,1)} %get-tuple-element.57), kind=kOutput, calls=%fused_computation.104 | convolution fusion | flops 3623878656 | bytes 13369344 | tf_op jit(solution)/shard_map/dot_general | solution.py:59
  227.4 2.3 fusion.10
  231.6 12.6 %collective-permute-done.8 = bf16[512,768]{1,0:T(8,128)(2,1)S(1)} collective-permute-done((bf16[512,768]{1,0:T(8,128)(2,1)S(1)}, bf16[512,768]{1,0:T(8,128)(2,1)S(1)}, u32[]{:S(2)}, u32[]{:S(2)}) %collective-permute-start.8) | collective-permute-done | bytes 786464 | tf_op jit(solution)/shard_map/ppermute | solution.py:419
  247.3 16.2 %all-to-all-start = ((bf16[8,96,1152]{2,1,0:T(8,128)(2,1)}), bf16[8,96,1152]{2,1,0:T(8,128)(2,1)}, u32[]{:S(2)}, u32[]{:S(2)}) async-start(bf16[8,96,1152]{2,1,0:T(8,128)(2,1)} %bitcast.41), calls=%async_computation | async-start | bytes 3538944 | tf_op jit(solution)/shard_map/all_to_all | solution.py:447
  264.9 36.4 %attend_back.2 = (bf16[1024,384]{1,0:T(8,128)(2,1)}, bf16[2048,384]{1,0:T(8,128)(2,1)}, bf16[2048,384]{1,0:T(8,128)(2,1)}) custom-call(bf16[1024,768]{1,0:T(8,128)(2,1)} %get-tuple-element.49.q_ref, bf16[1024,768]{1,0:T(8,128)(2,1)} %get-tuple-element.76.do_ref, bf16[1024,384]{1,0:T(8,128)(2,1)} %get-tuple-element.52.one_ref.o_ref, ...), custom_call_target="tpu_custom_call" | custom-call | flops 32212254720 | bytes 9437184 | tf_op jit(solution)/shard_map/attend_back/pallas_call | solution.py:190
  306.0 5.5 %all-to-all-start.1 = ((bf16[8,96,1024]{2,1,0:T(8,128)(2,1)}), bf16[8,96,1024]{2,1,0:T(8,128)(2,1)S(1)}, u32[]{:S(2)}, u32[]{:S(2)}) async-start(bf16[8,96,1024]{2,1,0:T(8,128)(2,1)} %bitcast.12), calls=%async_computation.1 | async-start | bytes 3145728 | tf_op jit(solution)/shard_map/all_to_all | solution.py:447
  311.4 36.6 %attend_back.3 = (bf16[1024,384]{1,0:T(8,128)(2,1)}, bf16[2048,384]{1,0:T(8,128)(2,1)}, bf16[2048,384]{1,0:T(8,128)(2,1)}) custom-call(bf16[1024,768]{1,0:T(8,128)(2,1)} %get-tuple-element.49.q_ref, bf16[1024,768]{1,0:T(8,128)(2,1)} %get-tuple-element.76.do_ref, bf16[1024,384]{1,0:T(8,128)(2,1)} %get-tuple-element.54.two_ref.o_ref, ...), custom_call_target="tpu_custom_call" | custom-call | flops 32212254720 | bytes 9437184 | tf_op jit(solution)/shard_map/attend_back/pallas_call | solution.py:190
  353.9 13.1 %finish.1 = (bf16[1024,2304]{1,0:T(8,128)(2,1)}, f32[1024,768]{1,0:T(8,128)}, f32[8,768]{1,0:T(8,128)}) custom-call(bf16[1024,768]{1,0:T(8,128)(2,1)} %pad_maximum_fusion.4.x_ref.refs_0_, f32[1024,768]{1,0:T(8,128)} %get-tuple-element.72.refs_1_, bf16[1024,384]{1,0:T(8,128)(2,1)} %get-tuple-element.69.refs_2_, bf16[2048,384]{1,0:T(8,128)(2,1)} %get-tuple-element.73.refs_3_, ...), custom_call_target="tpu_custom_call" | custom-call | flops 3623878656 | bytes 20447232 | tf_op jit(solution)/shard_map/finish/pallas_call | solution.py:394
  367.9 6.8 %fusion.17 = f32[768,2304]{1,0:T(8,128)S(1)} fusion(bf16[1024,768]{1,0:T(8,128)(2,1)} %get-tuple-element.71, bf16[1024,2304]{1,0:T(8,128)(2,1)} %get-tuple-element.82), kind=kOutput, calls=%fused_computation.107 | convolution fusion | flops 3623878656 | bytes 13369344 | tf_op jit(solution)/shard_map/dot_general | solution.py:59
  378.5 17.4 %collective-permute-done.12 = bf16[512,768]{1,0:T(8,128)(2,1)S(1)} collective-permute-done((bf16[512,768]{1,0:T(8,128)(2,1)S(1)}, bf16[512,768]{1,0:T(8,128)(2,1)S(1)}, u32[]{:S(2)}, u32[]{:S(2)}) %collective-permute-start.12) | collective-permute-done | bytes 786464 | tf_op jit(solution)/shard_map/ppermute | solution.py:419
  399.5 5.7 %all-to-all-start.2 = ((bf16[8,96,1280]{2,1,0:T(8,128)(2,1)}), bf16[8,96,1280]{2,1,0:T(8,128)(2,1)S(1)}, u32[]{:S(2)}, u32[]{:S(2)}) async-start(bf16[8,96,1280]{2,1,0:T(8,128)(2,1)} %bitcast.18), calls=%async_computation.2 | async-start | bytes 3932160 | tf_op jit(solution)/shard_map/all_to_all | solution.py:447
  408.3 4.2 collective-permute-done.17
  412.6 2.5 collective-permute-start.18
  418.8 3.9 collective-permute-done.15
  424.0 25.2 %all-to-all-done.2 = bf16[8,96,1280]{2,1,0:T(8,128)(2,1)S(1)} async-done(((bf16[8,96,1280]{2,1,0:T(8,128)(2,1)}), bf16[8,96,1280]{2,1,0:T(8,128)(2,1)S(1)}, u32[]{:S(2)}, u32[]{:S(2)}) %all-to-all-start.2) | async-done | bytes 1966112 | tf_op jit(solution)/shard_map/all_to_all | solution.py:447
  450.9 3.8 collective-permute-done.13
  454.8 3.6 collective-permute-start.14
  (160 shorter events, 81.3 us)
Async XLA Ops:
  7.2 52.9 %all-gather.5.cloned.1.call-start = ((), (), s32[]{:S(2)}) async-start(), calls=%async_computation.4 | async-start | bytes 2211840 | tf_op jit(solution)/shard_map/all_gather | solution.py:479
  10.8 120.6 %all-gather.3.cloned.1.call-start = ((), (), s32[]{:S(2)}) async-start(), calls=%async_computation.3 | async-start | bytes 3760128 | tf_op jit(solution)/shard_map/all_gather | solution.py:488
  60.1 23.8 %collective-permute-start.2 = (bf16[768,1280]{1,0:T(8,128)(2,1)}, bf16[768,1280]{1,0:T(8,128)(2,1)}, u32[]{:S(2)}, u32[]{:S(2)}) collective-permute-start(bf16[768,1280]{1,0:T(8,128)(2,1)} %all-gather.5.cloned.1.call-done), channel_id=1, source_target_pairs={{0,1},{1,0},{2,3},{3,2},{4,5},{5,4},{6,7},{7,6},{8,9},{9,8},{10,11... | collective-permute-start | bytes 5898248 | tf_op jit(solution)/shard_map/ppermute | solution.py:423
  63.0 19.5 %collective-permute-start.1 = (bf16[512,768]{1,0:T(8,128)(2,1)}, bf16[512,768]{1,0:T(8,128)(2,1)S(1)}, u32[]{:S(2)}, u32[]{:S(2)}) collective-permute-start(bf16[512,768]{1,0:T(8,128)(2,1)} %get-tuple-element.109), channel_id=1, source_target_pairs={{0,2},{2,0},{1,3},{3,1},{4,6},{6,4},{5,7},{7,5},{8,10},{10,8},{9,1... | collective-permute-start | bytes 2359304 | tf_op jit(solution)/shard_map/ppermute | solution.py:419
  98.5 3.9 collective-permute-start.3
  131.4 50.6 %collective-permute-start.5 = (bf16[768,2176]{1,0:T(8,128)(2,1)}, bf16[768,2176]{1,0:T(8,128)(2,1)S(1)}, u32[]{:S(2)}, u32[]{:S(2)}) collective-permute-start(bf16[768,2176]{1,0:T(8,128)(2,1)} %all-gather.3.cloned.1.call-done), channel_id=1, source_target_pairs={{0,1},{1,0},{2,3},{3,2},{4,5},{5,4},{6,7},{7,6},{8,9},{9,8},{10,11... | collective-permute-start | bytes 10027016 | tf_op jit(solution)/shard_map/ppermute | solution.py:423
  131.8 21.6 %collective-permute-start.4 = (bf16[1024,768]{1,0:T(8,128)(2,1)S(1)}, bf16[1024,768]{1,0:T(8,128)(2,1)S(1)}, u32[]{:S(2)}, u32[]{:S(2)}) collective-permute-start(bf16[1024,768]{1,0:T(8,128)(2,1)S(1)} %copy-done.11), channel_id=1, source_target_pairs={{0,1},{1,0},{2,3},{3,2},{4,5},{5,4},{6,7},{7,6},{8,9},{9,8},{10,11... | collective-permute-start | bytes 4718600 | tf_op jit(solution)/shard_map/ppermute | solution.py:423
  132.0 18.8 %collective-permute-start = (bf16[512,768]{1,0:T(8,128)(2,1)S(1)}, bf16[512,768]{1,0:T(8,128)(2,1)S(1)}, u32[]{:S(2)}, u32[]{:S(2)}) collective-permute-start(bf16[512,768]{1,0:T(8,128)(2,1)S(1)} %get-tuple-element.107), channel_id=1, source_target_pairs={{0,2},{2,0},{1,3},{3,1},{4,6},{6,4},{5,7},{7,5},{8,10},{10,8},{9,1... | collective-permute-start | bytes 2359304 | tf_op jit(solution)/shard_map/ppermute | solution.py:419
  224.1 21.4 %collective-permute-start.6 = (bf16[768,1152]{1,0:T(8,128)(2,1)S(1)}, bf16[768,1152]{1,0:T(8,128)(2,1)S(1)}, u32[]{:S(2)}, u32[]{:S(2)}) collective-permute-start(bf16[768,1152]{1,0:T(8,128)(2,1)S(1)} %select_convert_fusion.1), channel_id=1, source_target_pairs={{0,1},{1,0},{2,3},{3,2},{4,5},{5,4},{6,7},{7,6},{8,9},{9,8},{10,11... | collective-permute-start | bytes 5308424 | tf_op jit(solution)/shard_map/ppermute | solution.py:423
  225.5 18.7 %collective-permute-start.8 = (bf16[512,768]{1,0:T(8,128)(2,1)S(1)}, bf16[512,768]{1,0:T(8,128)(2,1)S(1)}, u32[]{:S(2)}, u32[]{:S(2)}) collective-permute-start(bf16[512,768]{1,0:T(8,128)(2,1)S(1)} %get-tuple-element.105), channel_id=1, source_target_pairs={{0,2},{2,0},{1,3},{3,1},{4,6},{6,4},{5,7},{7,5},{8,10},{10,8},{9,1... | collective-permute-start | bytes 2359304 | tf_op jit(solution)/shard_map/ppermute | solution.py:419
  247.3 58.7 %all-to-all-start = ((bf16[8,96,1152]{2,1,0:T(8,128)(2,1)}), bf16[8,96,1152]{2,1,0:T(8,128)(2,1)}, u32[]{:S(2)}, u32[]{:S(2)}) async-start(bf16[8,96,1152]{2,1,0:T(8,128)(2,1)} %bitcast.41), calls=%async_computation | async-start | bytes 3538944 | tf_op jit(solution)/shard_map/all_to_all | solution.py:447
  263.5 40.9 %collective-permute-start.7 = (bf16[768,1024]{1,0:T(8,128)(2,1)}, bf16[768,1024]{1,0:T(8,128)(2,1)S(1)}, u32[]{:S(2)}, u32[]{:S(2)}) collective-permute-start(bf16[768,1024]{1,0:T(8,128)(2,1)} %pad_maximum_fusion.5), channel_id=1, source_target_pairs={{0,1},{1,0},{2,3},{3,2},{4,5},{5,4},{6,7},{7,6},{8,9},{9,8},{10,11... | collective-permute-start | bytes 4718600 | tf_op jit(solution)/shard_map/ppermute | solution.py:423
  304.3 47.4 %collective-permute-start.9 = (bf16[1024,768]{1,0:T(8,128)(2,1)}, bf16[1024,768]{1,0:T(8,128)(2,1)}, u32[]{:S(2)}, u32[]{:S(2)}) collective-permute-start(bf16[1024,768]{1,0:T(8,128)(2,1)} %pad_maximum_fusion.6), channel_id=1, source_target_pairs={{0,1},{1,0},{2,3},{3,2},{4,5},{5,4},{6,7},{7,6},{8,9},{9,8},{10,11... | collective-permute-start | bytes 4718600 | tf_op jit(solution)/shard_map/ppermute | solution.py:423
  306.0 45.7 %all-to-all-start.1 = ((bf16[8,96,1024]{2,1,0:T(8,128)(2,1)}), bf16[8,96,1024]{2,1,0:T(8,128)(2,1)S(1)}, u32[]{:S(2)}, u32[]{:S(2)}) async-start(bf16[8,96,1024]{2,1,0:T(8,128)(2,1)} %bitcast.12), calls=%async_computation.1 | async-start | bytes 3145728 | tf_op jit(solution)/shard_map/all_to_all | solution.py:447
  349.9 4.0 collective-permute-start.10
  375.7 22.3 %collective-permute-start.11 = (bf16[768,1280]{1,0:T(8,128)(2,1)S(1)}, bf16[768,1280]{1,0:T(8,128)(2,1)S(1)}, u32[]{:S(2)}, u32[]{:S(2)}) collective-permute-start(bf16[768,1280]{1,0:T(8,128)(2,1)S(1)} %select_convert_fusion), channel_id=1, source_target_pairs={{0,1},{1,0},{2,3},{3,2},{4,5},{5,4},{6,7},{7,6},{8,9},{9,8},{10,11... | collective-permute-start | bytes 5898248 | tf_op jit(solution)/shard_map/ppermute | solution.py:423
  377.1 18.8 %collective-permute-start.12 = (bf16[512,768]{1,0:T(8,128)(2,1)S(1)}, bf16[512,768]{1,0:T(8,128)(2,1)S(1)}, u32[]{:S(2)}, u32[]{:S(2)}) collective-permute-start(bf16[512,768]{1,0:T(8,128)(2,1)S(1)} %slice.330), channel_id=1, source_target_pairs={{0,2},{2,0},{1,3},{3,1},{4,6},{6,4},{5,7},{7,5},{8,10},{10,8},{9,1... | collective-permute-start | bytes 2359304 | tf_op jit(solution)/shard_map/ppermute | solution.py:419
  399.5 49.7 %all-to-all-start.2 = ((bf16[8,96,1280]{2,1,0:T(8,128)(2,1)}), bf16[8,96,1280]{2,1,0:T(8,128)(2,1)S(1)}, u32[]{:S(2)}, u32[]{:S(2)}) async-start(bf16[8,96,1280]{2,1,0:T(8,128)(2,1)} %bitcast.18), calls=%async_computation.2 | async-start | bytes 3932160 | tf_op jit(solution)/shard_map/all_to_all | solution.py:447
  407.1 5.5 %collective-permute-start.17 = (bf16[96,1152]{1,0:T(8,128)(2,1)S(1)}, bf16[96,1152]{1,0:T(8,128)(2,1)S(1)}, u32[]{:S(2)}, u32[]{:S(2)}) collective-permute-start(bf16[96,1152]{1,0:T(8,128)(2,1)S(1)} %convert_element_type.119), channel_id=1, source_target_pairs={{0,2},{2,0},{1,3},{3,1},{4,6},{6,4},{5,7},{7,5},{8,10},{10,8},{9,1... | collective-permute-start | bytes 663560 | tf_op jit(solution)/shard_map/ppermute | solution.py:419
  412.6 3.6 collective-permute-start.18
  416.5 6.2 %collective-permute-start.15 = (bf16[96,1024]{1,0:T(8,128)(2,1)S(1)}, bf16[96,1024]{1,0:T(8,128)(2,1)S(1)}, u32[]{:S(2)}, u32[]{:S(2)}) collective-permute-start(bf16[96,1024]{1,0:T(8,128)(2,1)S(1)} %convert_element_type.114), channel_id=1, source_target_pairs={{0,2},{2,0},{1,3},{3,1},{4,6},{6,4},{5,7},{7,5},{8,10},{10,8},{9,1... | collective-permute-start | bytes 589832 | tf_op jit(solution)/shard_map/ppermute | solution.py:419
  422.8 28.1 %collective-permute-start.16 = (bf16[96,1024]{1,0:T(8,128)(2,1)S(1)}, bf16[96,1024]{1,0:T(8,128)(2,1)S(1)}, u32[]{:S(2)}, u32[]{:S(2)}) collective-permute-start(bf16[96,1024]{1,0:T(8,128)(2,1)S(1)} %add_convert_fusion.4), channel_id=1, source_target_pairs={{0,1},{1,0},{2,3},{3,2},{4,5},{5,4},{6,7},{7,6},{8,9},{9,8},{10,11... | collective-permute-start | bytes 589832 | tf_op jit(solution)/shard_map/ppermute | solution.py:423
  449.6 5.1 %collective-permute-start.13 = (bf16[96,1280]{1,0:T(8,128)(2,1)S(1)}, bf16[96,1280]{1,0:T(8,128)(2,1)S(1)}, u32[]{:S(2)}, u32[]{:S(2)}) collective-permute-start(bf16[96,1280]{1,0:T(8,128)(2,1)S(1)} %convert_element_type.109), channel_id=1, source_target_pairs={{0,2},{2,0},{1,3},{3,1},{4,6},{6,4},{5,7},{7,5},{8,10},{10,8},{9,1... | collective-permute-start | bytes 737288 | tf_op jit(solution)/shard_map/ppermute | solution.py:419
  454.8 5.1 %collective-permute-start.14 = (bf16[96,1280]{1,0:T(8,128)(2,1)S(1)}, bf16[96,1280]{1,0:T(8,128)(2,1)S(1)}, u32[]{:S(2)}, u32[]{:S(2)}) collective-permute-start(bf16[96,1280]{1,0:T(8,128)(2,1)S(1)} %add_convert_fusion.2), channel_id=1, source_target_pairs={{0,1},{1,0},{2,3},{3,2},{4,5},{5,4},{6,7},{7,6},{8,9},{9,8},{10,11... | collective-permute-start | bytes 737288 | tf_op jit(solution)/shard_map/ppermute | solution.py:423
  (19 other events, 180.3 us)
Sparse Core Ops, SparseCore 0:
  10.9 49.1 all-gather.4
  62.8 61.3 all-gather.2
